TPU v7x, 256 devices: a whole 4x4x8 slice. The times are simulated.
256 devices in a mesh: veh: 32 (over z, x), req: 8 (over y, core).
Axes of the slice: x: 4, y: 4, z: 8, core: 2. Of those that a mesh axis runs over, the one named last changes fastest.
Arguments:
- vehicle_emb: bfloat16 [32768, 128], P(('veh', 'req')), may hold values from -40 to 40
- request_emb: bfloat16 [32768, 128], P('req'), may hold values from -8 to 8
- request_feat: bfloat16 [32768, 256], P('req'), may hold values from -6 to 6
- log_supply: float32 [32768], P('veh'), may hold values from -1.2 to 1.2
- log_demand: float32 [32768], P('req'), may hold values from -1.2 to 1.2
Outputs:
- assigned: float32 [32768, 256], P(('veh', 'req'))
All inputs are finite; a program needn't handle non-finite values.
Results may differ from a plain program's by a relative error of at most 0.0017.
Values may be sent and summed in bfloat16 or wider, within the bound.
A program may use at most 64 MiB of HBM per device.

v0:
```python
import math

import jax
import jax.numpy as jnp
from jax import lax
from jax.sharding import PartitionSpec as P


def local(vehicle_emb, request_emb, request_feat, log_supply, log_demand):
    own_rows = lax.all_gather(vehicle_emb, "req", axis=0, tiled=True)
    row_count = own_rows.shape[0]
    block_rows = min(256, row_count)
    block_count = row_count // block_rows
    vehicle_blocks = own_rows.reshape(block_count, block_rows, own_rows.shape[1])
    score_scale = 3.0 / math.sqrt(own_rows.shape[1])
    request_count = request_emb.shape[0]

    def block_scores(vehicle_block):
        return (
            lax.dot_general(
                vehicle_block,
                request_emb,
                (((1,), (1,)), ((), ())),
                preferred_element_type=jnp.float32,
            )
            * score_scale
        )

    def column_pot(shift):
        shift_blocks = shift.reshape(block_count, block_rows)

        def column_step(state_pair, element):
            running, accrued = state_pair
            vehicle_block, shift_block = element
            logits = block_scores(vehicle_block) + shift_block[:, None]
            highest = jnp.maximum(running, jnp.max(logits, axis=0))
            accrued = accrued * jnp.exp(running - highest) + jnp.sum(
                jnp.exp(logits - highest[None, :]), axis=0
            )
            return ((highest, accrued), None)

        start_pair = (
            jnp.full((request_count,), -1e30, jnp.float32),
            jnp.zeros((request_count,), jnp.float32),
        )
        (highest, accrued), unused = lax.scan(
            column_step, start_pair, (vehicle_blocks, shift_blocks)
        )
        summit = lax.pmax(highest, "veh")
        accrued = lax.psum(accrued * jnp.exp(highest - summit), "veh")
        highest = summit
        return log_demand - (highest + jnp.log(accrued))

    demand_first = column_pot(jnp.zeros((row_count,), jnp.float32))

    def row_block(vehicle_block):
        logits = block_scores(vehicle_block) + demand_first[None, :]
        highest = jnp.max(logits, axis=1)
        return (highest, jnp.sum(jnp.exp(logits - highest[:, None]), axis=1))

    highest, accrued = lax.map(row_block, vehicle_blocks)
    highest = highest.reshape(row_count)
    accrued = accrued.reshape(row_count)
    summit = lax.pmax(highest, "req")
    accrued = lax.psum(accrued * jnp.exp(highest - summit), "req")
    highest = summit
    supply_pot = log_supply - (highest + jnp.log(accrued))
    demand_second = column_pot(supply_pot)

    def assign_block(vehicle_block):
        logits = block_scores(vehicle_block) + demand_second[None, :]
        block_peak = jnp.max(logits, axis=1)
        powers = jnp.exp(logits - block_peak[:, None])
        block_mass = jnp.sum(powers, axis=1)
        weights = powers.astype(jnp.bfloat16)
        block_feat = jnp.dot(weights, request_feat, preferred_element_type=jnp.float32)
        return (block_peak, block_mass, block_feat)

    peaks, masses, features = lax.map(assign_block, vehicle_blocks)
    peaks = peaks.reshape(row_count)
    masses = masses.reshape(row_count)
    features = features.reshape(row_count, request_feat.shape[1])
    summit = lax.pmax(peaks, "req")
    factor = jnp.exp(peaks - summit)
    own_feat, own_mass = (
        lax.psum_scatter(features * factor[:, None], "req", scatter_dimension=0, tiled=True),
        lax.psum_scatter(masses * factor, "req", scatter_dimension=0, tiled=True),
    )
    result = own_feat / own_mass[:, None]
    return result


def solution(mesh):
    in_specs = (P(("veh", "req"), None), P("req", None), P("req", None), P("veh"), P("req"))
    out_specs = P(("veh", "req"), None)
    return jax.shard_map(local, mesh=mesh, in_specs=in_specs, out_specs=out_specs, check_vma=False)
```

profile of v0, /device:TPU:1, one launch (start us, length us, event | category | flops | bytes accessed | tf_op | source)
XLA Modules:
  0.0 731.2 jit_solution(6975081202595240819)
XLA Ops:
  6.5 16.1 %all_gather.3 = bf16[1024,128]{1,0:T(8,128)(2,1)S(1)} all-gather(bf16[128,128]{1,0:T(8,128)(2,1)} %param.13), channel_id=1, replica_groups=mesh['veh'=32,'req'=8] {'req'}, dimensions={0}, use_global_device_ids=true | all-gather | bytes 294912 | tf_op jit(solution)/shard_map/all_gather | solution.py:10
  22.7 26.8 %while.54 = (s32[]{:T(128)}, f32[4096]{0:T(1024)S(1)}, f32[4096]{0:T(1024)S(1)}, bf16[4,256,128]{2,1,0:T(8,128)(2,1)S(1)}, bf16[4096,128]{1,0:T(8,128)(2,1)}, /*index=5*/s32[]{:T(128)}, s32[]{:T(128)}) while((s32[]{:T(128)}, f32[4096]{0:T(1024)S(1)}, f32[4096]{0:T(1024)S(1)}, bf16[4,256,128]{2,1,0:T(8,128)(2,1)S(1)}, ...), condition=%wide.region_3.4_spmd.clone, body=%wide.region_0.3_spmd.clone.sunk | while | flops 272650240 | bytes 9715804 | solution.py:46
  22.7 3.9 fusion.61
  26.5 2.8 exponential_reduce_fusion.7
  29.4 3.9 fusion.61
  33.2 2.8 exponential_reduce_fusion.7
  36.1 3.9 fusion.61
  39.9 2.8 exponential_reduce_fusion.7
  42.8 3.9 fusion.61
  46.6 2.8 exponential_reduce_fusion.7
  49.5 117.0 %pmax.28 = f32[4096]{0:T(1024)S(1)} all-reduce(f32[4096]{0:T(1024)S(1)} %get-tuple-element.143), channel_id=1, replica_groups=mesh['veh'=32,'req'=8] {'veh'}, use_global_device_ids=true, to_apply=%region_4.5 | all-reduce | flops 4096 | bytes 32768 | tf_op jit(solution)/shard_map/pmax | solution.py:49
  166.5 110.4 %psum.21 = f32[4096]{0:T(1024)S(1)} all-reduce(f32[4096]{0:T(1024)S(1)} %exponential_multiply_fusion.1), channel_id=1, replica_groups=mesh['veh'=32,'req'=8] {'veh'}, use_global_device_ids=true, to_apply=%region_5.6 | all-reduce | flops 4096 | bytes 32768 | tf_op jit(solution)/shard_map/psum | solution.py:50
  276.9 11.3 %while.52 = (s32[]{:T(128)}, f32[4,256]{1,0:T(4,128)S(1)}, f32[4,256]{1,0:T(4,128)S(1)}, bf16[4,256,128]{2,1,0:T(8,128)(2,1)S(1)}, bf16[4096,128]{1,0:T(8,128)(2...) while((s32[]{:T(128)}, f32[4,256]{1,0:T(4,128)S(1)}, f32[4,256]{1,0:T(4,128)S(1)}, ...), condition=%wide.region_9.10_spmd, body=%wide.region_6.9_spmd.sunk | while | flops 273677824 | bytes 9526369 | solution.py:61
  288.3 66.7 %pmax.29 = f32[1024]{0:T(1024)S(1)} all-reduce(f32[1024]{0:T(1024)S(1)} %bitcast.84), channel_id=1, replica_groups=mesh['veh'=32,'req'=8] {'req'}, use_global_device_ids=true, to_apply=%region_10.11 | all-reduce | flops 1024 | bytes 8192 | tf_op jit(solution)/shard_map/pmax | solution.py:64
  355.0 12.4 %psum.22 = f32[1024]{0:T(1024)S(1)} all-reduce(f32[1024]{0:T(1024)S(1)} %exponential_multiply_fusion.2), channel_id=1, replica_groups=mesh['veh'=32,'req'=8] {'req'}, use_global_device_ids=true, to_apply=%region_11.12 | all-reduce | flops 1024 | bytes 8192 | tf_op jit(solution)/shard_map/psum | solution.py:65
  367.5 27.0 %while.55 = (s32[]{:T(128)}, f32[4096]{0:T(1024)S(1)}, f32[4096]{0:T(1024)S(1)}, bf16[4,256,128]{2,1,0:T(8,128)(2,1)S(1)}, bf16[4096,128]{1,0:T(8,128)(2,1)}, /*index=5*/f32[4,256]{1,0:T(4,128)S(1)}, s32[]{:T(128)}, s32[]{:T(128)}) while((s32[]{:T(128)}, f32[4096]{0:T(1024)S(1)}, f32[4096]{0:T(1024)S(1)}, ...), condition=%wide.region_15.16_spmd.clone, body=%wide.region_12.15_spmd.clone.sunk | while | flops 273698816 | bytes 9718888 | solution.py:46
  367.5 4.0 fusion.64
  371.5 2.8 exponential_reduce_fusion.8
  374.4 3.9 fusion.64
  378.2 2.8 exponential_reduce_fusion.8
  381.1 3.9 fusion.64
  385.0 2.8 exponential_reduce_fusion.8
  387.8 3.9 fusion.64
  391.7 2.8 exponential_reduce_fusion.8
  394.5 109.9 %pmax.30 = f32[4096]{0:T(1024)S(1)} all-reduce(f32[4096]{0:T(1024)S(1)} %get-tuple-element.147), channel_id=1, replica_groups=mesh['veh'=32,'req'=8] {'veh'}, use_global_device_ids=true, to_apply=%region_16.17 | all-reduce | flops 4096 | bytes 32768 | tf_op jit(solution)/shard_map/pmax | solution.py:49
  504.4 110.3 %psum.23 = f32[4096]{0:T(1024)S(1)} all-reduce(f32[4096]{0:T(1024)S(1)} %exponential_multiply_fusion), channel_id=1, replica_groups=mesh['veh'=32,'req'=8] {'veh'}, use_global_device_ids=true, to_apply=%region_17.18 | all-reduce | flops 4096 | bytes 32768 | tf_op jit(solution)/shard_map/psum | solution.py:50
  614.8 14.6 %while.53 = (s32[]{:T(128)}, f32[4,256]{1,0:T(4,128)S(1)}, f32[4,256]{1,0:T(4,128)S(1)}, f32[4,256,256]{2,1,0:T(8,128)S(1)}, bf16[4,256,128]{2,1,0:T(8,128)(2,1)...) while((s32[]{:T(128)}, f32[4,256]{1,0:T(4,128)S(1)}, ...), condition=%wide.region_21.22_spmd, body=%wide.region_18.21_spmd.sunk | while | flops 812645888 | bytes 16081013 | solution.py:79
  622.1 2.0 fusion.57
  625.8 2.0 fusion.57
  629.4 67.6 %pmax.31 = f32[1024]{0:T(1024)S(1)} all-reduce(f32[1024]{0:T(1024)S(1)} %bitcast.82), channel_id=1, replica_groups=mesh['veh'=32,'req'=8] {'req'}, use_global_device_ids=true, to_apply=%region_22.23 | all-reduce | flops 1024 | bytes 8192 | tf_op jit(solution)/shard_map/pmax | solution.py:83
  699.5 12.4 %all-reduce = f32[1024]{0:T(1024)S(1)} all-reduce(f32[1024]{0:T(1024)S(1)} %get-tuple-element.241), channel_id=3, replica_groups=mesh['veh'=32,'req'=8] {'req'}, use_global_device_ids=true, to_apply=%region_24.25.clone | all-reduce | flops 1024 | bytes 8192
  712.0 10.7 %reduce-scatter.2.cloned.1.call-done = f32[128,256]{1,0:T(8,128)} async-done(((f32[1024,256]{1,0:T(8,128)}), f32[128,256]{1,0:T(8,128)}) %reduce-scatter.2.cloned.1.call-update) | async-done | bytes 131088 | tf_op jit(solution)/shard_map/reduce_scatter | solution.py:86
  (97 shorter events, 25.7 us)
Async XLA Ops:
  6.5 716.2 %reduce-scatter.2.cloned.1.call-start = ((), (), s32[]{:S(2)}) async-start(), calls=%async_computation.1 | async-start | bytes 1179648 | tf_op jit(solution)/shard_map/reduce_scatter | solution.py:86
  22.6 254.2 %copy-start.1 = (f32[4096]{0:T(1024)S(1)}, f32[4096]{0:T(1024)}, u32[]{:S(2)}) copy-start(f32[4096]{0:T(1024)} %param.17) | copy-start | bytes 49156
  276.9 90.5 %copy-start.2 = (f32[1024]{0:T(1024)S(1)}, f32[1024]{0:T(1024)}, u32[]{:S(2)}) copy-start(f32[1024]{0:T(1024)} %param.16) | copy-start | bytes 12292
  367.5 247.3 %copy-start = (bf16[4096,256]{1,0:T(8,128)(2,1)S(1)}, bf16[4096,256]{1,0:T(8,128)(2,1)}, u32[]{:S(2)}) copy-start(bf16[4096,256]{1,0:T(8,128)(2,1)} %param.15) | copy-start | bytes 6291460
  614.8 83.5 %copy-start.3 = (u32[256]{0:T(256)S(1)}, u32[256]{0:T(256)}, u32[]{:S(2)}) copy-start(u32[256]{0:T(256)} %constant.71) | copy-start | bytes 3076
Sparse Core Ops, SparseCore 0:
  698.4 24.2 reduce-scatter.1
where the time goes:
time: 734 us; the launch traced here: 731 us
  blocking collectives  623 us (85%)
  matrix products  50.6 us (7%)
  other arithmetic  31.1 us (4%)
  between operations  14.2 us (2%)
  waiting for transfers between devices  10.7 us (1%)
    pmax x2, blocking collectives, column_pot(): summit = lax.pmax(highest, 'veh')  227 us
    psum x2, blocking collectives, column_pot(): accrued = lax.psum(accrued * jnp.exp(highest - summit), 'veh')  221 us
    pmax x1, blocking collectives, local(): summit = lax.pmax(peaks, 'req')  67.6 us
    pmax x1, blocking collectives, local(): summit = lax.pmax(highest, 'req')  66.7 us
    dot_general x16, matrix products, block_scores(): lax.dot_general(vehicle_block, request_emb, (((1,), (1,)), ((), ())), pre...  47.3 us
    reduce_sum x8, other arithmetic, column_step(): jnp.sum(jnp.exp(logits - highest[None, :]), axis=0)  22.3 us
    all_gather x1, blocking collectives, local(): own_rows = lax.all_gather(vehicle_emb, 'req', axis=0, tiled=True)  16.1 us
  transfers between devices with their start and end apart: 1, of which 1 were waited for; matrix products, arithmetic and copies ran while one was open for 0% of the time, Pallas kernels for 0%

commit v1 on v0

v1 whole, which is shorter than its diff:
```python
import functools
import math

import jax
import jax.numpy as jnp
from jax import lax
from jax.experimental import pallas as pl
from jax.experimental.pallas import tpu as pltpu
from jax.sharding import PartitionSpec as P

MESH = pl.DeviceIdType.MESH
LOG2E = 1.4426950408889634
NX, NZ, NY = 4, 8, 4
NB = 8
BLK = 128
LANES = 128
NCHUNK = 4
TINY = 1e-30


def score_rows(v_all, r_t, z, top, slot, scale):
    width = 512
    v = v_all[slot]
    rows = pl.ds(pl.multiple_of(slot * BLK, BLK), BLK)

    def step(t, _):
        cols = pl.ds(pl.multiple_of(t * width, width), width)
        s = lax.dot_general(v, r_t[:, cols], (((1,), (0,)), ((), ())), preferred_element_type=jnp.float32) * scale
        z[rows, cols] = s
        top[:, cols] = jnp.maximum(top[:, cols], jnp.max(s.reshape(BLK // 8, 8, width), axis=0))
        return 0

    lax.fori_loop(0, z.shape[1] // width, step, 0)


def column_lse(z, top, c, cw):
    cols = pl.ds(c * cw, cw)
    peak = jnp.max(top[:, cols], axis=0, keepdims=True)
    rows = 32

    def step(t, acc):
        e = jnp.exp2(z[pl.ds(pl.multiple_of(t * rows, rows), rows), cols] - peak)
        return acc + jnp.sum(e.reshape(rows // 8, 8, cw), axis=0)

    acc = lax.fori_loop(0, z.shape[0] // rows, step, jnp.zeros((8, cw), jnp.float32), unroll=2)
    return peak + jnp.log(jnp.sum(acc, axis=0, keepdims=True)) * LOG2E


def row_pass(z, d, m, s, c, cw):
    rows = 16
    kk = cw // LANES

    def step(t, _):
        rr = pl.ds(pl.multiple_of(t * rows, rows), rows)
        ys = [z[rr, pl.ds(c * cw + k * LANES, LANES)] + d[:, pl.ds(c * cw + k * LANES, LANES)] for k in range(kk)]
        peak = functools.reduce(jnp.maximum, ys)
        total = None
        for k in range(kk):
            e = jnp.exp2(ys[k] - peak)
            z[rr, pl.ds(c * cw + k * LANES, LANES)] = e
            total = e if total is None else total + e
        m[c, rr, :] = peak
        s[c, rr, :] = total
        return 0

    lax.fori_loop(0, z.shape[0] // rows, step, 0, unroll=2)


def row_totals(m, s, out):
    def step(g, _):
        rr = pl.ds(pl.multiple_of(g * BLK, BLK), BLK)
        peak = functools.reduce(jnp.maximum, [m[c, rr, :] for c in range(NCHUNK)])
        total = sum(s[c, rr, :] * jnp.exp2(m[c, rr, :] - peak) for c in range(NCHUNK))
        pt, tt = peak.T, total.T
        top = jnp.max(pt, axis=0, keepdims=True)
        out[g] = top + jnp.log(jnp.sum(tt * jnp.exp2(pt - top), axis=0, keepdims=True)) * LOG2E
        return 0

    lax.fori_loop(0, NB, step, 0)


def row_scales(m, sp):
    def step(g, _):
        rr = pl.ds(pl.multiple_of(g * BLK, BLK), BLK)
        col = jnp.broadcast_to(sp[g], (BLK, LANES)).T
        for c in range(NCHUNK):
            m[c, rr, :] = jnp.exp2(m[c, rr, :] + col)
        return 0

    lax.fori_loop(0, NB, step, 0)


def column_sum(z, u, c, cw):
    rows = 32
    kk = cw // LANES

    def step(t, accs):
        rr = pl.ds(pl.multiple_of(t * rows, rows), rows)
        ut = u[c, rr, :]
        return tuple(
            a + jnp.sum((z[rr, pl.ds(c * cw + k * LANES, LANES)] * ut).reshape(rows // 8, 8, LANES), axis=0)
            for k, a in enumerate(accs)
        )

    zero = tuple(jnp.zeros((8, LANES), jnp.float32) for _ in range(kk))
    accs = lax.fori_loop(0, z.shape[0] // rows, step, zero, unroll=2)
    return jnp.concatenate([jnp.sum(a, axis=0, keepdims=True) for a in accs], axis=1)


def weight_pass(z, u, gain, tm, ms, c, cw):
    rows = 16
    kk = cw // LANES

    def step(t, _):
        rr = pl.ds(pl.multiple_of(t * rows, rows), rows)
        ut = u[c, rr, :]
        peak = total = None
        for k in range(kk):
            cols = pl.ds(c * cw + k * LANES, LANES)
            e = z[rr, cols] * ut * gain[:, cols]
            z[rr, cols] = e
            peak = e if peak is None else jnp.maximum(peak, e)
            total = e if total is None else total + e
        if c > 0:
            peak, total = jnp.maximum(peak, tm[rr, :]), total + ms[rr, :]
        tm[rr, :] = peak
        ms[rr, :] = total
        return 0

    lax.fori_loop(0, z.shape[0] // rows, step, 0, unroll=2)


def block_features(z, tm, feat, row0, rows):
    rr = pl.ds(pl.multiple_of(row0, rows), rows)
    peak = jnp.maximum(jnp.max(tm[rr, :], axis=1, keepdims=True), TINY)
    w = (z[rr, :] * (1.0 / peak)).astype(jnp.bfloat16)
    return jnp.dot(w, feat[...], preferred_element_type=jnp.float32) * peak


def lse_parts(parts):
    top = jnp.max(parts, axis=0)
    return top + jnp.log(jnp.sum(jnp.exp2(parts - top[None]), axis=0)) * LOG2E


def kernel(v_hbm, r_hbm, feat_hbm, sup_hbm, dem_hbm, out,
           v_all, r, r_t, feat, sup, dem, z, top, d, gain, m, s, tm, ms,
           xbuf, zbuf, rowbuf, massown, massbuf, sp, fpart, fmate, fsend, frecv,
           load_sem, ag_send, ag_recv, x_send, x_recv, z_send, z_recv, row_sem, mass_sem,
           mate_send, mate_recv, f_send, f_recv):
    me, b = lax.axis_index("veh"), lax.axis_index("req")
    zc, xc = me // NX, lax.rem(me, NX)
    y, core = b // 2, lax.rem(b, 2)
    cw = z.shape[1] // NCHUNK
    scale = 3.0 / math.sqrt(v_hbm.shape[1]) * LOG2E

    def x_peer(k):
        return (zc * NX + lax.rem(xc + k, NX), b)

    def z_peer(k):
        return (lax.rem(zc + k, NZ) * NX + xc, b)

    def req_peer(k):
        return (me, lax.rem(b + k, NB))

    loads = [
        pltpu.make_async_copy(v_hbm, v_all.at[b], load_sem.at[0]),
        pltpu.make_async_copy(r_hbm, r, load_sem.at[1]),
        pltpu.make_async_copy(sup_hbm, sup, load_sem.at[2]),
        pltpu.make_async_copy(dem_hbm, dem, load_sem.at[3]),
        pltpu.make_async_copy(feat_hbm, feat, load_sem.at[4]),
    ]
    for load in loads:
        load.start()
    barrier = pltpu.get_barrier_semaphore()
    for k in range(1, NX):
        pl.semaphore_signal(barrier, inc=1, device_id=x_peer(k), device_id_type=MESH)
    for k in range(1, NZ):
        pl.semaphore_signal(barrier, inc=1, device_id=z_peer(k), device_id_type=MESH)
    for k in range(1, NB):
        pl.semaphore_signal(barrier, inc=1, device_id=req_peer(k), device_id_type=MESH)
    top[...] = jnp.full(top.shape, -3e38, jnp.float32)
    loads[1].wait()

    def flip(t, _):
        w = 512
        r_t[:, pl.ds(pl.multiple_of(t * w, w), w)] = r[pl.ds(pl.multiple_of(t * w, w), w), :].T
        return 0

    lax.fori_loop(0, r.shape[0] // 512, flip, 0)
    loads[0].wait()
    pl.semaphore_wait(barrier, NX + NZ + NB - 3)

    order = (1, 2, 6, 7, 3, 5, 4)
    gathers = []
    for k in order:
        copy = pltpu.make_async_remote_copy(
            v_all.at[b], v_all.at[b], ag_send.at[k], ag_recv.at[NB - k], device_id=req_peer(k), device_id_type=MESH)
        copy.start()
        gathers.append(copy)
    score_rows(v_all, r_t, z, top, b, scale)
    for k in order:
        slot = lax.rem(b + k, NB)
        pltpu.make_async_copy(v_all.at[slot], v_all.at[slot], ag_recv.at[k]).wait()
        score_rows(v_all, r_t, z, top, slot, scale)

    def x_start(a, c):
        for k in range(1, NX):
            pltpu.make_async_remote_copy(
                xbuf.at[a, c, NX - 1], xbuf.at[a, c, NX - 1 - k], x_send.at[a, c], x_recv.at[a, c],
                device_id=x_peer(k), device_id_type=MESH).start()

    def z_start(a, c):
        for k in range(1, NZ):
            pltpu.make_async_remote_copy(
                zbuf.at[a, c, NZ - 1], zbuf.at[a, c, NZ - 1 - k], z_send.at[a, c], z_recv.at[a, c],
                device_id=z_peer(k), device_id_type=MESH).start()

    def all_of(buf, n, sem):
        pltpu.make_async_copy(buf.at[pl.ds(0, n)], buf.at[pl.ds(0, n)], sem).wait()

    loads[2].wait()
    loads[3].wait()
    for c in range(NCHUNK):
        xbuf[0, c, NX - 1] = column_lse(z, top, c, cw)
        x_start(0, c)
    for c in range(NCHUNK):
        all_of(xbuf.at[0, c], NX - 1, x_recv.at[0, c])
        zbuf[0, c, NZ - 1] = lse_parts(xbuf[0, c])
        z_start(0, c)
    for c in range(NCHUNK):
        all_of(zbuf.at[0, c], NZ - 1, z_recv.at[0, c])
        cols = pl.ds(c * cw, cw)
        d[:, cols] = dem[:, cols] * LOG2E - lse_parts(zbuf[0, c])
        row_pass(z, d, m, s, c, cw)

    row_totals(m, s, rowbuf.at[NB - 1])
    for k in range(1, NB):
        pltpu.make_async_remote_copy(
            rowbuf.at[NB - 1], rowbuf.at[NB - 1 - k], row_sem.at[0], row_sem.at[1],
            device_id=req_peer(k), device_id_type=MESH).start()
    all_of(rowbuf, NB - 1, row_sem.at[1])
    sp[...] = sup[...] * LOG2E - lse_parts(rowbuf[...])
    row_scales(m, sp)

    for c in range(NCHUNK):
        xbuf[1, c, NX - 1] = column_sum(z, m, c, cw)
        x_start(1, c)
    for c in range(NCHUNK):
        all_of(xbuf.at[1, c], NX - 1, x_recv.at[1, c])
        zbuf[1, c, NZ - 1] = jnp.sum(xbuf[1, c], axis=0)
        z_start(1, c)
    for c in range(NCHUNK):
        all_of(zbuf.at[1, c], NZ - 1, z_recv.at[1, c])
        cols = pl.ds(c * cw, cw)
        gain[:, cols] = jnp.exp2(dem[:, cols] * LOG2E) / jnp.sum(zbuf[1, c], axis=0)
        weight_pass(z, m, gain, tm, ms, c, cw)

    def mass_step(g, _):
        rr = pl.ds(pl.multiple_of(g * BLK, BLK), BLK)
        massown[g] = jnp.sum(ms[rr, :].T, axis=0, keepdims=True)
        return 0

    lax.fori_loop(0, NB, mass_step, 0)
    for k in range(1, NB):
        pltpu.make_async_remote_copy(
            massown.at[lax.rem(b + k, NB)], massbuf.at[NB - 1 - k], mass_sem.at[0], mass_sem.at[1],
            device_id=req_peer(k), device_id_type=MESH).start()
    massbuf[NB - 1] = massown[b]

    loads[4].wait()
    steps = (2, 1, 3, 0)

    def mate_copy(i):
        return pltpu.make_async_remote_copy(
            fpart.at[i, 1 - core], fmate.at[i], mate_send.at[i], mate_recv.at[i],
            device_id=(me, y * 2 + 1 - core), device_id_type=MESH)

    def out_copy(i):
        return pltpu.make_async_remote_copy(
            fsend.at[i], frecv.at[i], f_send.at[i], f_recv.at[i],
            device_id=(me, lax.rem(y + steps[i], NY) * 2 + core), device_id_type=MESH)

    def pass_on(i):
        mate_copy(i).wait_recv()
        fsend[i] = (fpart[i, core] + fmate[i]).astype(jnp.bfloat16)
        out_copy(i).start()

    for i, step in enumerate(steps):
        row0 = lax.rem(y + step, NY) * 2 * BLK
        fpart[i] = block_features(z, tm, feat, row0, 2 * BLK).reshape(2, BLK, feat.shape[1])
        mate_copy(i).start()
        if i > 0:
            pass_on(i - 1)
    all_of(massbuf, NB - 1, mass_sem.at[1])
    mass = jnp.sum(massbuf[...], axis=0)
    inv = 1.0 / jnp.broadcast_to(mass, (BLK, LANES)).T
    last = len(steps) - 1
    mate_copy(last).wait_recv()
    total = fpart[last, core] + fmate[last]
    for i in range(last):
        out_copy(i).wait_recv()
        total = total + frecv[i].astype(jnp.float32)
    for k in range(feat.shape[1] // LANES):
        out[:, k * LANES:(k + 1) * LANES] = total[:, k * LANES:(k + 1) * LANES] * inv

    for copy in gathers:
        copy.wait_send()
    for a in range(2):
        for c in range(NCHUNK):
            all_of(xbuf.at[a, c], NX - 1, x_send.at[a, c])
            all_of(zbuf.at[a, c], NZ - 1, z_send.at[a, c])
    all_of(rowbuf, NB - 1, row_sem.at[0])
    all_of(massbuf, NB - 1, mass_sem.at[0])
    for i in range(len(steps)):
        mate_copy(i).wait_send()
    for i in range(last):
        out_copy(i).wait_send()


def local(vehicle_emb, request_emb, request_feat, log_supply, log_demand):
    rows, cols, width = BLK * NB, request_emb.shape[0], request_feat.shape[1]
    cw = cols // NCHUNK
    f32, bf16 = jnp.float32, jnp.bfloat16
    dma = pltpu.SemaphoreType.DMA
    scratch = [
        pltpu.VMEM((NB, BLK, vehicle_emb.shape[1]), bf16),
        pltpu.VMEM(request_emb.shape, bf16),
        pltpu.VMEM(request_emb.shape[::-1], bf16),
        pltpu.VMEM(request_feat.shape, bf16),
        pltpu.VMEM((NB, 1, LANES), f32),
        pltpu.VMEM((1, cols), f32),
        pltpu.VMEM((rows, cols), f32),
        pltpu.VMEM((8, cols), f32),
        pltpu.VMEM((1, cols), f32),
        pltpu.VMEM((1, cols), f32),
        pltpu.VMEM((NCHUNK, rows, LANES), f32),
        pltpu.VMEM((NCHUNK, rows, LANES), f32),
        pltpu.VMEM((rows, LANES), f32),
        pltpu.VMEM((rows, LANES), f32),
        pltpu.VMEM((2, NCHUNK, NX, 1, cw), f32),
        pltpu.VMEM((2, NCHUNK, NZ, 1, cw), f32),
        pltpu.VMEM((NB, NB, 1, LANES), f32),
        pltpu.VMEM((NB, 1, LANES), f32),
        pltpu.VMEM((NB, 1, LANES), f32),
        pltpu.VMEM((NB, 1, LANES), f32),
        pltpu.VMEM((NY, 2, BLK, width), f32),
        pltpu.VMEM((NY, BLK, width), f32),
        pltpu.VMEM((NY - 1, BLK, width), bf16),
        pltpu.VMEM((NY - 1, BLK, width), bf16),
        dma((5,)), dma((NB,)), dma((NB,)),
        dma((2, NCHUNK)), dma((2, NCHUNK)), dma((2, NCHUNK)), dma((2, NCHUNK)),
        dma((2,)), dma((2,)),
        dma((NY,)), dma((NY,)), dma((NY - 1,)), dma((NY - 1,)),
    ]
    return pl.pallas_call(
        kernel,
        out_shape=jax.ShapeDtypeStruct((BLK, width), f32),
        in_specs=[pl.BlockSpec(memory_space=pl.ANY)] * 5,
        out_specs=pl.BlockSpec(memory_space=pltpu.VMEM),
        scratch_shapes=scratch,
        compiler_params=pltpu.CompilerParams(
            collective_id=0, has_side_effects=True, vmem_limit_bytes=56 * 2**20),
        cost_estimate=pl.CostEstimate(
            flops=2 * rows * cols * (vehicle_emb.shape[1] + width), bytes_accessed=4 * 2**20,
            transcendentals=2 * rows * cols),
        name="sinkhorn_assign",
    )(vehicle_emb, request_emb, request_feat, log_supply.reshape(NB, 1, LANES), log_demand.reshape(1, cols))


def solution(mesh):
    in_specs = (P(("veh", "req"), None), P("req", None), P("req", None), P("veh"), P("req"))
    out_specs = P(("veh", "req"), None)
    return jax.shard_map(local, mesh=mesh, in_specs=in_specs, out_specs=out_specs, check_vma=False)
```

time: 734 us -> 67.8 us (0.09)
  blocking collectives: 623 us -> 0 us
  Pallas kernels: 0 us -> 66.2 us
  matrix products: 50.6 us -> 0 us
  other arithmetic: 31.1 us -> 0 us
  between operations: 14.2 us -> 0.01 us
  waiting for transfers between devices: 10.7 us -> 0 us
    pmax x4 -> x0, blocking collectives: 361 us -> none  [the longest x2 227 us: column_pot(): summit = lax.pmax(highest, 'veh')]
    psum x3 -> x0, blocking collectives: 233 us -> none  [the longest x2 221 us: column_pot(): accrued = lax.psum(accrued * jnp.exp(highest - summit), 'veh')]
    pallas_call x0 -> x1, Pallas kernels: none -> 66.2 us  [local(): pl.pallas_call(kernel, out_shape=jax.ShapeDtypeStruct((BLK, width), f32),...]
    dot_general x20 -> x0, matrix products: 50.6 us -> none  [the longest x16 47.3 us: block_scores(): lax.dot_general(vehicle_block, request_emb, (((1,), (1,)), ((), ())), pre...]
    reduce_sum x16 -> x0, other arithmetic: 28 us -> none  [the longest x8 22.3 us: column_step(): jnp.sum(jnp.exp(logits - highest[None, :]), axis=0)]
    all_gather x1 -> x0, blocking collectives: 16.1 us -> none  [local(): own_rows = lax.all_gather(vehicle_emb, 'req', axis=0, tiled=True)]
    unnamed x1 -> x0, blocking collectives: 12.4 us -> none
    reduce_scatter x1 -> x0, waiting for transfers between devices: 10.7 us -> none  [local(): lax.psum_scatter(features * factor[:, None], 'req', scatter_dimension=0,...]
  transfers between devices with their start and end apart: 1 -> 0, of which waited for: 1 -> 0; matrix products, arithmetic and copies ran while one was open for 0% -> 0% of each run, Pallas kernels for 0% -> 0%
where the time goes in v1:
time: 67.8 us; the launch traced here: 67.7 us
  Pallas kernels  66.2 us (98%)
  local copies, waits for them, and re-layouts  1.57 us (2%)
    pallas_call x1, Pallas kernels, local(): pl.pallas_call(kernel, out_shape=jax.ShapeDtypeStruct((BLK, width), f32),...  66.2 us
    unnamed x1, local copies, waits for them, and re-layouts  1.57 us

profile of v1, /device:TPU:1, one launch (start us, length us, event | category | flops | bytes accessed | tf_op | source)
XLA Modules:
  0.0 67.7 jit_solution(17719469734594695257)
XLA Ops:
  0.0 66.2 %sinkhorn_assign.1 = f32[128,256]{1,0:T(8,128)} custom-call(bf16[128,128]{1,0:T(8,128)(2,1)} %v_hbm.1, bf16[4096,128]{1,0:T(8,128)(2,1)} %r_hbm.1, bf16[4096,256]{1,0:T(8,128)(2,1)} %feat_hbm.1, f32[8,1,128]{2,1,0:T(1,128)} %bitcast.3, f32[1,4096]{1,0:T(1,128)} %bitcast.2), custom_call_target="tpu_custom_call" | custom-call | flops 3221225472 | bytes 4194304 | tf_op jit(solution)/shard_map/sinkhorn_assign/pallas_call | solution.py:355
  66.2 1.6 %copy.7 = f32[128,256]{1,0:T(8,128)} copy(f32[128,256]{1,0:T(8,128)} %sinkhorn_assign.1) | data formatting | bytes 262144

commit v2 on v1

--- a/solution.py
+++ b/solution.py
@@ -18,36 +18,32 @@
 TINY = 1e-30
 
 
-def score_rows(v_all, r_t, z, top, slot, scale):
+def score_rows(v_all, r_t, z, top, acc, slot, scale, first):
     width = 512
     v = v_all[slot]
     rows = pl.ds(pl.multiple_of(slot * BLK, BLK), BLK)
-
-    def step(t, _):
-        cols = pl.ds(pl.multiple_of(t * width, width), width)
+    for t in range(z.shape[1] // width):
+        cols = pl.ds(t * width, width)
         s = lax.dot_general(v, r_t[:, cols], (((1,), (0,)), ((), ())), preferred_element_type=jnp.float32) * scale
         z[rows, cols] = s
-        top[:, cols] = jnp.maximum(top[:, cols], jnp.max(s.reshape(BLK // 8, 8, width), axis=0))
-        return 0
-
-    lax.fori_loop(0, z.shape[1] // width, step, 0)
-
-
-def column_lse(z, top, c, cw):
-    cols = pl.ds(c * cw, cw)
-    peak = jnp.max(top[:, cols], axis=0, keepdims=True)
+        s = s.reshape(BLK // 8, 8, width)
+        peak = jnp.max(s, axis=0)
+        if not first:
+            old = top[:, cols]
+            peak = jnp.maximum(old, peak)
+        e = jnp.sum(jnp.exp2(s - peak[None]), axis=0)
+        top[:, cols] = peak
+        acc[:, cols] = e if first else acc[:, cols] * jnp.exp2(old - peak) + e
+
+
+def column_lse(top, acc):
+    t = top[...]
+    peak = jnp.max(t, axis=0, keepdims=True)
+    return peak + jnp.log(jnp.sum(acc[...] * jnp.exp2(t - peak), axis=0, keepdims=True)) * LOG2E
+
+
+def row_pass(z, d, w, m, s, c, cw):
     rows = 32
-
-    def step(t, acc):
-        e = jnp.exp2(z[pl.ds(pl.multiple_of(t * rows, rows), rows), cols] - peak)
-        return acc + jnp.sum(e.reshape(rows // 8, 8, cw), axis=0)
-
-    acc = lax.fori_loop(0, z.shape[0] // rows, step, jnp.zeros((8, cw), jnp.float32), unroll=2)
-    return peak + jnp.log(jnp.sum(acc, axis=0, keepdims=True)) * LOG2E
-
-
-def row_pass(z, d, m, s, c, cw):
-    rows = 16
     kk = cw // LANES
 
     def step(t, _):
@@ -57,7 +53,7 @@
         total = None
         for k in range(kk):
             e = jnp.exp2(ys[k] - peak)
-            z[rr, pl.ds(c * cw + k * LANES, LANES)] = e
+            w[rr, pl.ds(c * cw + k * LANES, LANES)] = e
             total = e if total is None else total + e
         m[c, rr, :] = peak
         s[c, rr, :] = total
@@ -67,30 +63,24 @@
 
 
 def row_totals(m, s, out):
-    def step(g, _):
-        rr = pl.ds(pl.multiple_of(g * BLK, BLK), BLK)
+    for g in range(NB):
+        rr = pl.ds(g * BLK, BLK)
         peak = functools.reduce(jnp.maximum, [m[c, rr, :] for c in range(NCHUNK)])
         total = sum(s[c, rr, :] * jnp.exp2(m[c, rr, :] - peak) for c in range(NCHUNK))
         pt, tt = peak.T, total.T
         top = jnp.max(pt, axis=0, keepdims=True)
         out[g] = top + jnp.log(jnp.sum(tt * jnp.exp2(pt - top), axis=0, keepdims=True)) * LOG2E
-        return 0
-
-    lax.fori_loop(0, NB, step, 0)
 
 
 def row_scales(m, sp):
-    def step(g, _):
-        rr = pl.ds(pl.multiple_of(g * BLK, BLK), BLK)
+    for g in range(NB):
+        rr = pl.ds(g * BLK, BLK)
         col = jnp.broadcast_to(sp[g], (BLK, LANES)).T
         for c in range(NCHUNK):
             m[c, rr, :] = jnp.exp2(m[c, rr, :] + col)
-        return 0
-
-    lax.fori_loop(0, NB, step, 0)
-
-
-def column_sum(z, u, c, cw):
+
+
+def column_sum(w, u, c, cw):
     rows = 32
     kk = cw // LANES
 
@@ -98,27 +88,27 @@
         rr = pl.ds(pl.multiple_of(t * rows, rows), rows)
         ut = u[c, rr, :]
         return tuple(
-            a + jnp.sum((z[rr, pl.ds(c * cw + k * LANES, LANES)] * ut).reshape(rows // 8, 8, LANES), axis=0)
+            a + jnp.sum((w[rr, pl.ds(c * cw + k * LANES, LANES)] * ut).reshape(rows // 8, 8, LANES), axis=0)
             for k, a in enumerate(accs)
         )
 
     zero = tuple(jnp.zeros((8, LANES), jnp.float32) for _ in range(kk))
-    accs = lax.fori_loop(0, z.shape[0] // rows, step, zero, unroll=2)
+    accs = lax.fori_loop(0, w.shape[0] // rows, step, zero, unroll=4)
     return jnp.concatenate([jnp.sum(a, axis=0, keepdims=True) for a in accs], axis=1)
 
 
-def weight_pass(z, u, gain, tm, ms, c, cw):
-    rows = 16
+def weight_pass(w, u, gain, t, tm, ms, c, cw):
+    rows = 64
     kk = cw // LANES
 
-    def step(t, _):
-        rr = pl.ds(pl.multiple_of(t * rows, rows), rows)
+    def step(i, _):
+        rr = pl.ds(pl.multiple_of(i * rows, rows), rows)
         ut = u[c, rr, :]
         peak = total = None
         for k in range(kk):
             cols = pl.ds(c * cw + k * LANES, LANES)
-            e = z[rr, cols] * ut * gain[:, cols]
-            z[rr, cols] = e
+            e = w[rr, cols] * ut * gain[:, cols]
+            t[rr, cols] = e
             peak = e if peak is None else jnp.maximum(peak, e)
             total = e if total is None else total + e
         if c > 0:
@@ -127,14 +117,14 @@
         ms[rr, :] = total
         return 0
 
-    lax.fori_loop(0, z.shape[0] // rows, step, 0, unroll=2)
-
-
-def block_features(z, tm, feat, row0, rows):
+    lax.fori_loop(0, w.shape[0] // rows, step, 0)
+
+
+def block_features(t, tm, feat, row0, rows):
     rr = pl.ds(pl.multiple_of(row0, rows), rows)
     peak = jnp.maximum(jnp.max(tm[rr, :], axis=1, keepdims=True), TINY)
-    w = (z[rr, :] * (1.0 / peak)).astype(jnp.bfloat16)
-    return jnp.dot(w, feat[...], preferred_element_type=jnp.float32) * peak
+    weights = (t[rr, :] * (1.0 / peak)).astype(jnp.bfloat16)
+    return jnp.dot(weights, feat[...], preferred_element_type=jnp.float32) * peak
 
 
 def lse_parts(parts):
@@ -143,9 +133,9 @@
 
 
 def kernel(v_hbm, r_hbm, feat_hbm, sup_hbm, dem_hbm, out,
-           v_all, r, r_t, feat, sup, dem, z, top, d, gain, m, s, tm, ms,
-           xbuf, zbuf, rowbuf, massown, massbuf, sp, fpart, fmate, fsend, frecv,
-           load_sem, ag_send, ag_recv, x_send, x_recv, z_send, z_recv, row_sem, mass_sem,
+           v_all, r, r_t, feat, sup, dem, z, w, top, acc, d, gain, m, s, tm, ms,
+           xwide, xbuf, zbuf, rowbuf, massown, massbuf, sp, fpart, fmate, fsend, frecv,
+           load_sem, ag_send, ag_recv, xw_sem, x_send, x_recv, z_send, z_recv, row_sem, mass_sem,
            mate_send, mate_recv, f_send, f_recv):
     me, b = lax.axis_index("veh"), lax.axis_index("req")
     zc, xc = me // NX, lax.rem(me, NX)
@@ -178,35 +168,34 @@
         pl.semaphore_signal(barrier, inc=1, device_id=z_peer(k), device_id_type=MESH)
     for k in range(1, NB):
         pl.semaphore_signal(barrier, inc=1, device_id=req_peer(k), device_id_type=MESH)
-    top[...] = jnp.full(top.shape, -3e38, jnp.float32)
     loads[1].wait()
 
     def flip(t, _):
-        w = 512
-        r_t[:, pl.ds(pl.multiple_of(t * w, w), w)] = r[pl.ds(pl.multiple_of(t * w, w), w), :].T
+        part = pl.ds(pl.multiple_of(t * 512, 512), 512)
+        r_t[:, part] = r[part, :].T
         return 0
 
     lax.fori_loop(0, r.shape[0] // 512, flip, 0)
     loads[0].wait()
     pl.semaphore_wait(barrier, NX + NZ + NB - 3)
 
-    order = (1, 2, 6, 7, 3, 5, 4)
+    order = (1, 7, 2, 6, 3, 5, 4)
     gathers = []
     for k in order:
         copy = pltpu.make_async_remote_copy(
             v_all.at[b], v_all.at[b], ag_send.at[k], ag_recv.at[NB - k], device_id=req_peer(k), device_id_type=MESH)
         copy.start()
         gathers.append(copy)
-    score_rows(v_all, r_t, z, top, b, scale)
+    score_rows(v_all, r_t, z, top, acc, b, scale, True)
     for k in order:
         slot = lax.rem(b + k, NB)
         pltpu.make_async_copy(v_all.at[slot], v_all.at[slot], ag_recv.at[k]).wait()
-        score_rows(v_all, r_t, z, top, slot, scale)
-
-    def x_start(a, c):
+        score_rows(v_all, r_t, z, top, acc, slot, scale, False)
+
+    def x_start(c):
         for k in range(1, NX):
             pltpu.make_async_remote_copy(
-                xbuf.at[a, c, NX - 1], xbuf.at[a, c, NX - 1 - k], x_send.at[a, c], x_recv.at[a, c],
+                xbuf.at[c, NX - 1], xbuf.at[c, NX - 1 - k], x_send.at[c], x_recv.at[c],
                 device_id=x_peer(k), device_id_type=MESH).start()
 
     def z_start(a, c):
@@ -220,18 +209,20 @@
 
     loads[2].wait()
     loads[3].wait()
-    for c in range(NCHUNK):
-        xbuf[0, c, NX - 1] = column_lse(z, top, c, cw)
-        x_start(0, c)
-    for c in range(NCHUNK):
-        all_of(xbuf.at[0, c], NX - 1, x_recv.at[0, c])
-        zbuf[0, c, NZ - 1] = lse_parts(xbuf[0, c])
+    xwide[NX - 1] = column_lse(top, acc)
+    for k in range(1, NX):
+        pltpu.make_async_remote_copy(
+            xwide.at[NX - 1], xwide.at[NX - 1 - k], xw_sem.at[0], xw_sem.at[1],
+            device_id=x_peer(k), device_id_type=MESH).start()
+    all_of(xwide, NX - 1, xw_sem.at[1])
+    for c in range(NCHUNK):
+        zbuf[0, c, NZ - 1] = lse_parts(xwide[:, :, pl.ds(c * cw, cw)])
         z_start(0, c)
     for c in range(NCHUNK):
         all_of(zbuf.at[0, c], NZ - 1, z_recv.at[0, c])
         cols = pl.ds(c * cw, cw)
         d[:, cols] = dem[:, cols] * LOG2E - lse_parts(zbuf[0, c])
-        row_pass(z, d, m, s, c, cw)
+        row_pass(z, d, w, m, s, c, cw)
 
     row_totals(m, s, rowbuf.at[NB - 1])
     for k in range(1, NB):
@@ -243,17 +234,17 @@
     row_scales(m, sp)
 
     for c in range(NCHUNK):
-        xbuf[1, c, NX - 1] = column_sum(z, m, c, cw)
-        x_start(1, c)
-    for c in range(NCHUNK):
-        all_of(xbuf.at[1, c], NX - 1, x_recv.at[1, c])
-        zbuf[1, c, NZ - 1] = jnp.sum(xbuf[1, c], axis=0)
+        xbuf[c, NX - 1] = column_sum(w, m, c, cw)
+        x_start(c)
+    for c in range(NCHUNK):
+        all_of(xbuf.at[c], NX - 1, x_recv.at[c])
+        zbuf[1, c, NZ - 1] = jnp.sum(xbuf[c], axis=0)
         z_start(1, c)
     for c in range(NCHUNK):
         all_of(zbuf.at[1, c], NZ - 1, z_recv.at[1, c])
         cols = pl.ds(c * cw, cw)
         gain[:, cols] = jnp.exp2(dem[:, cols] * LOG2E) / jnp.sum(zbuf[1, c], axis=0)
-        weight_pass(z, m, gain, tm, ms, c, cw)
+        weight_pass(w, m, gain, z, tm, ms, c, cw)
 
     def mass_step(g, _):
         rr = pl.ds(pl.multiple_of(g * BLK, BLK), BLK)
@@ -305,9 +296,10 @@
 
     for copy in gathers:
         copy.wait_send()
-    for a in range(2):
-        for c in range(NCHUNK):
-            all_of(xbuf.at[a, c], NX - 1, x_send.at[a, c])
+    all_of(xwide, NX - 1, xw_sem.at[0])
+    for c in range(NCHUNK):
+        all_of(xbuf.at[c], NX - 1, x_send.at[c])
+        for a in range(2):
             all_of(zbuf.at[a, c], NZ - 1, z_send.at[a, c])
     all_of(rowbuf, NB - 1, row_sem.at[0])
     all_of(massbuf, NB - 1, mass_sem.at[0])
@@ -330,6 +322,8 @@
         pltpu.VMEM((NB, 1, LANES), f32),
         pltpu.VMEM((1, cols), f32),
         pltpu.VMEM((rows, cols), f32),
+        pltpu.VMEM((rows, cols), f32),
+        pltpu.VMEM((8, cols), f32),
         pltpu.VMEM((8, cols), f32),
         pltpu.VMEM((1, cols), f32),
         pltpu.VMEM((1, cols), f32),
@@ -337,7 +331,8 @@
         pltpu.VMEM((NCHUNK, rows, LANES), f32),
         pltpu.VMEM((rows, LANES), f32),
         pltpu.VMEM((rows, LANES), f32),
-        pltpu.VMEM((2, NCHUNK, NX, 1, cw), f32),
+        pltpu.VMEM((NX, 1, cols), f32),
+        pltpu.VMEM((NCHUNK, NX, 1, cw), f32),
         pltpu.VMEM((2, NCHUNK, NZ, 1, cw), f32),
         pltpu.VMEM((NB, NB, 1, LANES), f32),
         pltpu.VMEM((NB, 1, LANES), f32),
@@ -348,7 +343,7 @@
         pltpu.VMEM((NY - 1, BLK, width), bf16),
         pltpu.VMEM((NY - 1, BLK, width), bf16),
         dma((5,)), dma((NB,)), dma((NB,)),
-        dma((2, NCHUNK)), dma((2, NCHUNK)), dma((2, NCHUNK)), dma((2, NCHUNK)),
+        dma((2,)), dma((NCHUNK,)), dma((NCHUNK,)), dma((2, NCHUNK)), dma((2, NCHUNK)),
         dma((2,)), dma((2,)),
         dma((NY,)), dma((NY,)), dma((NY - 1,)), dma((NY - 1,)),
     ]

time: 67.8 us -> 58.1 us (0.86)
  Pallas kernels: 66.2 us -> 56.4 us
    pallas_call x1, Pallas kernels: 66.2 us -> 56.4 us  [local(): pl.pallas_call(kernel, out_shape=jax.ShapeDtypeStruct((BLK, width), f32),...]
where the time goes in v2:
time: 58.1 us; the launch traced here: 58 us
  Pallas kernels  56.4 us (97%)
  local copies, waits for them, and re-layouts  1.57 us (3%)
    pallas_call x1, Pallas kernels, local(): pl.pallas_call(kernel, out_shape=jax.ShapeDtypeStruct((BLK, width), f32),...  56.4 us
    unnamed x1, local copies, waits for them, and re-layouts  1.57 us

profile of v2, /device:TPU:1, one launch (start us, length us, event | category | flops | bytes accessed | tf_op | source)
XLA Modules:
  0.0 58.0 jit_solution(9125128865902699448)
XLA Ops:
  0.0 56.4 %sinkhorn_assign.1 = f32[128,256]{1,0:T(8,128)} custom-call(bf16[128,128]{1,0:T(8,128)(2,1)} %v_hbm.1, bf16[4096,128]{1,0:T(8,128)(2,1)} %r_hbm.1, bf16[4096,256]{1,0:T(8,128)(2,1)} %feat_hbm.1, f32[8,1,128]{2,1,0:T(1,128)} %bitcast.3, f32[1,4096]{1,0:T(1,128)} %bitcast.2), custom_call_target="tpu_custom_call" | custom-call | flops 3221225472 | bytes 4194304 | tf_op jit(solution)/shard_map/sinkhorn_assign/pallas_call | solution.py:350
  56.4 1.6 %copy.7 = f32[128,256]{1,0:T(8,128)} copy(f32[128,256]{1,0:T(8,128)} %sinkhorn_assign.1) | data formatting | bytes 262144

commit v3 on v2

v3 whole, which is shorter than its diff:
```python
import functools
import math

import jax
import jax.numpy as jnp
from jax import lax
from jax.experimental import pallas as pl
from jax.experimental.pallas import tpu as pltpu
from jax.sharding import PartitionSpec as P

MESH = pl.DeviceIdType.MESH
LOG2E = 1.4426950408889634
NX, NZ, NY = 4, 8, 4
NB = 8
BLK = 128
LANES = 128
NCHUNK = 4
TINY = 1e-30


def score_rows(v_all, r, z, top, acc, slot, scale, first=False, start=0, stop=None):
    width = 512
    v = v_all[slot]
    rows = pl.ds(pl.multiple_of(slot * BLK, BLK), BLK)
    for c in range(start, stop or z.shape[1], width):
        cols = pl.ds(c, width)
        s = lax.dot_general(v, r[cols, :], (((1,), (1,)), ((), ())), preferred_element_type=jnp.float32) * scale
        z[rows, cols] = s
        s = s.reshape(BLK // 8, 8, width)
        peak = jnp.max(s, axis=0)
        if not first:
            old = top[:, cols]
            peak = jnp.maximum(old, peak)
        e = jnp.sum(jnp.exp2(s - peak[None]), axis=0)
        top[:, cols] = peak
        acc[:, cols] = e if first else acc[:, cols] * jnp.exp2(old - peak) + e


def column_lse(top, acc, cols):
    t = top[:, cols]
    peak = jnp.max(t, axis=0, keepdims=True)
    return peak + jnp.log(jnp.sum(acc[:, cols] * jnp.exp2(t - peak), axis=0, keepdims=True)) * LOG2E


def row_pass(z, d, w, m, s, c, cw):
    rows = 64
    kk = cw // LANES

    def step(t, _):
        rr = pl.ds(pl.multiple_of(t * rows, rows), rows)
        ys = [z[rr, pl.ds(c * cw + k * LANES, LANES)] + d[:, pl.ds(c * cw + k * LANES, LANES)] for k in range(kk)]
        peak = functools.reduce(jnp.maximum, ys)
        total = None
        for k in range(kk):
            e = jnp.exp2(ys[k] - peak)
            w[rr, pl.ds(c * cw + k * LANES, LANES)] = e
            total = e if total is None else total + e
        m[c, rr, :] = peak
        s[c, rr, :] = total
        return 0

    lax.fori_loop(0, z.shape[0] // rows, step, 0, unroll=2)


def row_totals(m, s, out):
    for g in range(NB):
        rr = pl.ds(g * BLK, BLK)
        peak = functools.reduce(jnp.maximum, [m[c, rr, :] for c in range(NCHUNK)])
        total = sum(s[c, rr, :] * jnp.exp2(m[c, rr, :] - peak) for c in range(NCHUNK))
        pt, tt = peak.T, total.T
        top = jnp.max(pt, axis=0, keepdims=True)
        out[g] = top + jnp.log(jnp.sum(tt * jnp.exp2(pt - top), axis=0, keepdims=True)) * LOG2E


def spread(sp, col):
    for g in range(NB):
        col[pl.ds(g * BLK, BLK), :] = jnp.broadcast_to(sp[g], (BLK, LANES)).T


def column_sum(w, u, col, c, cw):
    u[c] = jnp.exp2(u[c] + col[...])
    rows = 32
    kk = cw // LANES

    def step(t, accs):
        rr = pl.ds(pl.multiple_of(t * rows, rows), rows)
        ut = u[c, rr, :]
        return tuple(
            a + jnp.sum((w[rr, pl.ds(c * cw + k * LANES, LANES)] * ut).reshape(rows // 8, 8, LANES), axis=0)
            for k, a in enumerate(accs)
        )

    zero = tuple(jnp.zeros((8, LANES), jnp.float32) for _ in range(kk))
    accs = lax.fori_loop(0, w.shape[0] // rows, step, zero, unroll=4)
    return jnp.concatenate([jnp.sum(a, axis=0, keepdims=True) for a in accs], axis=1)


def weight_pass(w, u, gain, t, tm, ms, c, cw):
    rows = 64
    kk = cw // LANES

    def step(i, _):
        rr = pl.ds(pl.multiple_of(i * rows, rows), rows)
        ut = u[c, rr, :]
        peak = total = None
        for k in range(kk):
            cols = pl.ds(c * cw + k * LANES, LANES)
            e = w[rr, cols] * ut * gain[:, cols]
            t[rr, cols] = e
            peak = e if peak is None else jnp.maximum(peak, e)
            total = e if total is None else total + e
        if c > 0:
            peak, total = jnp.maximum(peak, tm[rr, :]), total + ms[rr, :]
        tm[rr, :] = peak
        ms[rr, :] = total
        return 0

    lax.fori_loop(0, w.shape[0] // rows, step, 0)


def block_features(t, tm, feat, row0, rows):
    rr = pl.ds(pl.multiple_of(row0, rows), rows)
    peak = jnp.maximum(jnp.max(tm[rr, :], axis=1, keepdims=True), TINY)
    weights = (t[rr, :] * (1.0 / peak)).astype(jnp.bfloat16)
    return jnp.dot(weights, feat[...], preferred_element_type=jnp.float32) * peak


def lse_parts(parts):
    top = jnp.max(parts, axis=0)
    return top + jnp.log(jnp.sum(jnp.exp2(parts - top[None]), axis=0)) * LOG2E


def kernel(v_hbm, r_hbm, feat_hbm, sup_hbm, dem_hbm, out,
           v_all, r, feat, sup, dem, z, w, top, acc, d, gain, m, s, tm, ms,
           col, xbuf, zbuf, rowbuf, massown, massbuf, sp, fgive, fkeep, fmate, fsend, frecv,
           load_sem, ag_send, ag_recv, relay, x_send, x_recv, z_send, z_recv, row_sem, mass_sem,
           mate_send, mate_recv, f_send, f_recv):
    me, b = lax.axis_index("veh"), lax.axis_index("req")
    zc, xc = me // NX, lax.rem(me, NX)
    y, core = b // 2, lax.rem(b, 2)
    cw = z.shape[1] // NCHUNK
    scale = 3.0 / math.sqrt(v_hbm.shape[1]) * LOG2E

    def x_peer(k):
        return (zc * NX + lax.rem(xc + k, NX), b)

    def z_peer(k):
        return (lax.rem(zc + k, NZ) * NX + xc, b)

    def req_peer(k):
        return (me, lax.rem(b + k, NB))

    def at(dy, dc):
        return lax.rem(y + dy, NY) * 2 + lax.rem(core + dc, 2)

    loads = [
        pltpu.make_async_copy(v_hbm, v_all.at[b], load_sem.at[0]),
        pltpu.make_async_copy(r_hbm, r, load_sem.at[1]),
        pltpu.make_async_copy(sup_hbm, sup, load_sem.at[2]),
        pltpu.make_async_copy(dem_hbm, dem, load_sem.at[3]),
        pltpu.make_async_copy(feat_hbm, feat, load_sem.at[4]),
    ]
    sent = []
    loads[0].start()
    barrier = pltpu.get_barrier_semaphore()
    near_z = (z_peer(1), z_peer(NZ - 1))
    for peer in [req_peer(k) for k in range(1, NB)] + [x_peer(k) for k in range(1, NX)] + list(near_z):
        pl.semaphore_signal(barrier, inc=1, device_id=peer, device_id_type=MESH)
    for load in loads[1:]:
        load.start()
    loads[0].wait()
    pl.semaphore_wait(barrier, NB - 1 + NX - 1 + 2)

    def tell(i):
        for peer in near_z:
            pl.semaphore_signal(relay.at[i], inc=1, device_id=peer, device_id_type=MESH)

    def told(i):
        pl.semaphore_wait(relay.at[i], 2)

    for dy, dc in ((2, 0), (2, 1), (1, 0), (3, 0), (1, 1), (3, 1), (0, 1)):
        copy = pltpu.make_async_remote_copy(
            v_all.at[b], v_all.at[b], ag_send.at[dy, dc], ag_recv.at[(NY - dy) % NY, dc],
            device_id=(me, at(dy, dc)), device_id_type=MESH)
        copy.start()
        sent.append(copy.wait_send)
    tell(0)

    def arrival(dy, dc):
        slot = at(dy, dc)
        pltpu.make_async_copy(v_all.at[slot], v_all.at[slot], ag_recv.at[dy, dc]).wait()
        return slot

    loads[1].wait()
    score_rows(v_all, r, z, top, acc, b, scale, first=True)
    for i, (dy, dc) in enumerate(((0, 1), (1, 0), (3, 0), (1, 1), (3, 1))):
        score_rows(v_all, r, z, top, acc, arrival(dy, dc), scale)
        if i < 3:
            told(i)
        if i < 2:
            tell(i + 1)
    far = (arrival(2, 0), arrival(2, 1))

    def x_start(a, c):
        for k in range(1, NX):
            pltpu.make_async_remote_copy(
                xbuf.at[a, c, NX - 1], xbuf.at[a, c, NX - 1 - k], x_send.at[a, c], x_recv.at[a, c],
                device_id=x_peer(k), device_id_type=MESH).start()
        sent.append(lambda: all_of(xbuf.at[a, c], NX - 1, x_send.at[a, c]))

    def z_start(a, c):
        for k in range(1, NZ):
            pltpu.make_async_remote_copy(
                zbuf.at[a, c, NZ - 1], zbuf.at[a, c, NZ - 1 - k], z_send.at[a, c], z_recv.at[a, c],
                device_id=z_peer(k), device_id_type=MESH).start()
        sent.append(lambda: all_of(zbuf.at[a, c], NZ - 1, z_send.at[a, c]))

    def all_of(buf, n, sem):
        pltpu.make_async_copy(buf.at[pl.ds(0, n)], buf.at[pl.ds(0, n)], sem).wait()

    loads[2].wait()
    loads[3].wait()
    for c in range(NCHUNK):
        for slot in far:
            score_rows(v_all, r, z, top, acc, slot, scale, start=c * cw, stop=(c + 1) * cw)
        xbuf[0, c, NX - 1] = column_lse(top, acc, pl.ds(c * cw, cw))
        x_start(0, c)
    for c in range(NCHUNK):
        all_of(xbuf.at[0, c], NX - 1, x_recv.at[0, c])
        zbuf[0, c, NZ - 1] = lse_parts(xbuf[0, c])
        z_start(0, c)
    for c in range(NCHUNK):
        all_of(zbuf.at[0, c], NZ - 1, z_recv.at[0, c])
        cols = pl.ds(c * cw, cw)
        d[:, cols] = dem[:, cols] * LOG2E - lse_parts(zbuf[0, c])
        row_pass(z, d, w, m, s, c, cw)

    row_totals(m, s, rowbuf.at[NB - 1])
    for k in range(1, NB):
        pltpu.make_async_remote_copy(
            rowbuf.at[NB - 1], rowbuf.at[NB - 1 - k], row_sem.at[0], row_sem.at[1],
            device_id=req_peer(k), device_id_type=MESH).start()
    sent.append(lambda: all_of(rowbuf, NB - 1, row_sem.at[0]))
    all_of(rowbuf, NB - 1, row_sem.at[1])
    sp[...] = sup[...] * LOG2E - lse_parts(rowbuf[...])
    spread(sp, col)

    for c in range(NCHUNK):
        xbuf[1, c, NX - 1] = column_sum(w, m, col, c, cw)
        x_start(1, c)
    for c in range(NCHUNK):
        all_of(xbuf.at[1, c], NX - 1, x_recv.at[1, c])
        zbuf[1, c, NZ - 1] = jnp.sum(xbuf[1, c], axis=0)
        z_start(1, c)
    for c in range(NCHUNK):
        all_of(zbuf.at[1, c], NZ - 1, z_recv.at[1, c])
        cols = pl.ds(c * cw, cw)
        gain[:, cols] = jnp.exp2(dem[:, cols] * LOG2E) / jnp.sum(zbuf[1, c], axis=0)
        weight_pass(w, m, gain, z, tm, ms, c, cw)

    def masses():
        for g in range(NB):
            massown[g] = jnp.sum(ms[pl.ds(g * BLK, BLK), :].T, axis=0, keepdims=True)
        for k in range(1, NB):
            pltpu.make_async_remote_copy(
                massown.at[lax.rem(b + k, NB)], massbuf.at[NB - 1 - k], mass_sem.at[0], mass_sem.at[1],
                device_id=req_peer(k), device_id_type=MESH).start()
        sent.append(lambda: all_of(massbuf, NB - 1, mass_sem.at[0]))
        massbuf[NB - 1] = massown[b]

    def mate_copy(i):
        return pltpu.make_async_remote_copy(
            fgive.at[i], fmate.at[i], mate_send.at[i], mate_recv.at[i],
            device_id=(me, at(0, 1)), device_id_type=MESH)

    def out_copy(i):
        return pltpu.make_async_remote_copy(
            fsend.at[i], frecv.at[i], f_send.at[i], f_recv.at[i],
            device_id=(me, at(steps[i], 0)), device_id_type=MESH)

    def give(i):
        fgive[i] = block_features(z, tm, feat, at(steps[i], 1) * BLK, BLK)
        mate_copy(i).start()
        sent.append(mate_copy(i).wait_send)

    def keep(i):
        fkeep[i] = block_features(z, tm, feat, at(steps[i], 0) * BLK, BLK)

    def pass_on(i):
        mate_copy(i).wait_recv()
        fsend[i] = (fkeep[i] + fmate[i]).astype(jnp.bfloat16)
        out_copy(i).start()
        sent.append(out_copy(i).wait_send)

    steps = (2, 1, 3, 0)
    last = len(steps) - 1
    loads[4].wait()
    give(0)
    give(1)
    give(2)
    keep(0)
    masses()
    keep(1)
    pass_on(0)
    keep(2)
    pass_on(1)
    give(3)
    pass_on(2)
    keep(3)
    all_of(massbuf, NB - 1, mass_sem.at[1])
    mass = jnp.sum(massbuf[...], axis=0)
    inv = 1.0 / jnp.broadcast_to(mass, (BLK, LANES)).T
    mate_copy(last).wait_recv()
    total = fkeep[last] + fmate[last]
    for i in (1, 2, 0):
        out_copy(i).wait_recv()
        total = total + frecv[i].astype(jnp.float32)
    for k in range(feat.shape[1] // LANES):
        out[:, k * LANES:(k + 1) * LANES] = total[:, k * LANES:(k + 1) * LANES] * inv

    for wait in sent:
        wait()


def local(vehicle_emb, request_emb, request_feat, log_supply, log_demand):
    rows, cols, width = BLK * NB, request_emb.shape[0], request_feat.shape[1]
    cw = cols // NCHUNK
    f32, bf16 = jnp.float32, jnp.bfloat16
    dma = pltpu.SemaphoreType.DMA
    scratch = [
        pltpu.VMEM((NB, BLK, vehicle_emb.shape[1]), bf16),
        pltpu.VMEM(request_emb.shape, bf16),
        pltpu.VMEM(request_feat.shape, bf16),
        pltpu.VMEM((NB, 1, LANES), f32),
        pltpu.VMEM((1, cols), f32),
        pltpu.VMEM((rows, cols), f32),
        pltpu.VMEM((rows, cols), f32),
        pltpu.VMEM((8, cols), f32),
        pltpu.VMEM((8, cols), f32),
        pltpu.VMEM((1, cols), f32),
        pltpu.VMEM((1, cols), f32),
        pltpu.VMEM((NCHUNK, rows, LANES), f32),
        pltpu.VMEM((NCHUNK, rows, LANES), f32),
        pltpu.VMEM((rows, LANES), f32),
        pltpu.VMEM((rows, LANES), f32),
        pltpu.VMEM((rows, LANES), f32),
        pltpu.VMEM((2, NCHUNK, NX, 1, cw), f32),
        pltpu.VMEM((2, NCHUNK, NZ, 1, cw), f32),
        pltpu.VMEM((NB, NB, 1, LANES), f32),
        pltpu.VMEM((NB, 1, LANES), f32),
        pltpu.VMEM((NB, 1, LANES), f32),
        pltpu.VMEM((NB, 1, LANES), f32),
        pltpu.VMEM((NY, BLK, width), f32),
        pltpu.VMEM((NY, BLK, width), f32),
        pltpu.VMEM((NY, BLK, width), f32),
        pltpu.VMEM((NY - 1, BLK, width), bf16),
        pltpu.VMEM((NY - 1, BLK, width), bf16),
        dma((5,)), dma((NY, 2)), dma((NY, 2)), pltpu.SemaphoreType.REGULAR((3,)),
        dma((2, NCHUNK)), dma((2, NCHUNK)), dma((2, NCHUNK)), dma((2, NCHUNK)),
        dma((2,)), dma((2,)),
        dma((NY,)), dma((NY,)), dma((NY - 1,)), dma((NY - 1,)),
    ]
    return pl.pallas_call(
        kernel,
        out_shape=jax.ShapeDtypeStruct((BLK, width), f32),
        in_specs=[pl.BlockSpec(memory_space=pl.ANY)] * 5,
        out_specs=pl.BlockSpec(memory_space=pltpu.VMEM),
        scratch_shapes=scratch,
        compiler_params=pltpu.CompilerParams(
            collective_id=0, has_side_effects=True, vmem_limit_bytes=56 * 2**20),
        cost_estimate=pl.CostEstimate(
            flops=2 * rows * cols * (vehicle_emb.shape[1] + width), bytes_accessed=4 * 2**20,
            transcendentals=2 * rows * cols),
        name="sinkhorn_assign",
    )(vehicle_emb, request_emb, request_feat, log_supply.reshape(NB, 1, LANES), log_demand.reshape(1, cols))


def solution(mesh):
    in_specs = (P(("veh", "req"), None), P("req", None), P("req", None), P("veh"), P("req"))
    out_specs = P(("veh", "req"), None)
    return jax.shard_map(local, mesh=mesh, in_specs=in_specs, out_specs=out_specs, check_vma=False)
```

time: 58.1 us -> 55.8 us (0.960)
  Pallas kernels: 56.4 us -> 54 us
    pallas_call x1, Pallas kernels: 56.4 us -> 54 us  [local(): pl.pallas_call(kernel, out_shape=jax.ShapeDtypeStruct((BLK, width), f32),...]
where the time goes in v3:
time: 55.8 us; the launch traced here: 55.6 us
  Pallas kernels  54 us (97%)
  local copies, waits for them, and re-layouts  1.57 us (3%)
    pallas_call x1, Pallas kernels, local(): pl.pallas_call(kernel, out_shape=jax.ShapeDtypeStruct((BLK, width), f32),...  54 us
    unnamed x1, local copies, waits for them, and re-layouts  1.57 us

profile of v3, /device:TPU:1, one launch (start us, length us, event | category | flops | bytes accessed | tf_op | source)
XLA Modules:
  0.0 55.6 jit_solution(7537259392174374294)
XLA Ops:
  0.0 54.0 %sinkhorn_assign.1 = f32[128,256]{1,0:T(8,128)} custom-call(bf16[128,128]{1,0:T(8,128)(2,1)} %v_hbm.1, bf16[4096,128]{1,0:T(8,128)(2,1)} %r_hbm.1, bf16[4096,256]{1,0:T(8,128)(2,1)} %feat_hbm.1, f32[8,1,128]{2,1,0:T(1,128)} %bitcast.3, f32[1,4096]{1,0:T(1,128)} %bitcast.2), custom_call_target="tpu_custom_call" | custom-call | flops 3221225472 | bytes 4194304 | tf_op jit(solution)/shard_map/sinkhorn_assign/pallas_call | solution.py:363
  54.0 1.6 %copy.7 = f32[128,256]{1,0:T(8,128)} copy(f32[128,256]{1,0:T(8,128)} %sinkhorn_assign.1) | data formatting | bytes 262144

commit v4 on v3

--- a/solution.py
+++ b/solution.py
@@ -18,15 +18,15 @@
 TINY = 1e-30
 
 
-def score_rows(v_all, r, z, top, acc, slot, scale, first=False, start=0, stop=None):
+def score_rows(v_all, r, z, top, acc, slot, n, scale, first=False, start=0, stop=None):
     width = 512
-    v = v_all[slot]
-    rows = pl.ds(pl.multiple_of(slot * BLK, BLK), BLK)
+    v = v_all[slot:slot + n].reshape(n * BLK, v_all.shape[2])
+    rows = pl.ds(slot * BLK, n * BLK)
     for c in range(start, stop or z.shape[1], width):
         cols = pl.ds(c, width)
         s = lax.dot_general(v, r[cols, :], (((1,), (1,)), ((), ())), preferred_element_type=jnp.float32) * scale
         z[rows, cols] = s
-        s = s.reshape(BLK // 8, 8, width)
+        s = s.reshape(n * BLK // 8, 8, width)
         peak = jnp.max(s, axis=0)
         if not first:
             old = top[:, cols]
@@ -62,19 +62,19 @@
     lax.fori_loop(0, z.shape[0] // rows, step, 0, unroll=2)
 
 
-def row_totals(m, s, out):
-    for g in range(NB):
-        rr = pl.ds(g * BLK, BLK)
+def row_totals(m, s, out, place):
+    for q in range(NB):
+        rr = pl.ds(q * BLK, BLK)
         peak = functools.reduce(jnp.maximum, [m[c, rr, :] for c in range(NCHUNK)])
         total = sum(s[c, rr, :] * jnp.exp2(m[c, rr, :] - peak) for c in range(NCHUNK))
         pt, tt = peak.T, total.T
         top = jnp.max(pt, axis=0, keepdims=True)
-        out[g] = top + jnp.log(jnp.sum(tt * jnp.exp2(pt - top), axis=0, keepdims=True)) * LOG2E
-
-
-def spread(sp, col):
-    for g in range(NB):
-        col[pl.ds(g * BLK, BLK), :] = jnp.broadcast_to(sp[g], (BLK, LANES)).T
+        out[place(q)] = top + jnp.log(jnp.sum(tt * jnp.exp2(pt - top), axis=0, keepdims=True)) * LOG2E
+
+
+def spread(sp, col, place):
+    for q in range(NB):
+        col[pl.ds(q * BLK, BLK), :] = jnp.broadcast_to(sp[place(q)], (BLK, LANES)).T
 
 
 def column_sum(w, u, col, c, cw):
@@ -95,20 +95,20 @@
     return jnp.concatenate([jnp.sum(a, axis=0, keepdims=True) for a in accs], axis=1)
 
 
-def weight_pass(w, u, gain, t, tm, ms, c, cw):
+def weight_pass(w, u, gain, tm, ms, c, cw):
     rows = 64
     kk = cw // LANES
 
     def step(i, _):
         rr = pl.ds(pl.multiple_of(i * rows, rows), rows)
-        ut = u[c, rr, :]
         peak = total = None
         for k in range(kk):
             cols = pl.ds(c * cw + k * LANES, LANES)
-            e = w[rr, cols] * ut * gain[:, cols]
-            t[rr, cols] = e
+            e = w[rr, cols] * gain[:, cols]
             peak = e if peak is None else jnp.maximum(peak, e)
             total = e if total is None else total + e
+        ut = u[c, rr, :]
+        peak, total = peak * ut, total * ut
         if c > 0:
             peak, total = jnp.maximum(peak, tm[rr, :]), total + ms[rr, :]
         tm[rr, :] = peak
@@ -118,11 +118,16 @@
     lax.fori_loop(0, w.shape[0] // rows, step, 0)
 
 
-def block_features(t, tm, feat, row0, rows):
-    rr = pl.ds(pl.multiple_of(row0, rows), rows)
+def block_features(w, u, gain, tm, feat, packed, row0, rows, cw):
+    rr = pl.ds(row0, rows)
     peak = jnp.maximum(jnp.max(tm[rr, :], axis=1, keepdims=True), TINY)
-    weights = (t[rr, :] * (1.0 / peak)).astype(jnp.bfloat16)
-    return jnp.dot(weights, feat[...], preferred_element_type=jnp.float32) * peak
+    inv = 1.0 / peak
+    for c in range(NCHUNK):
+        a = u[c, rr, :] * inv
+        for k in range(cw // LANES):
+            cols = pl.ds(c * cw + k * LANES, LANES)
+            packed[:, cols] = (w[rr, cols] * a * gain[:, cols]).astype(jnp.bfloat16)
+    return jnp.dot(packed[...], feat[...], preferred_element_type=jnp.float32) * peak
 
 
 def lse_parts(parts):
@@ -132,7 +137,7 @@
 
 def kernel(v_hbm, r_hbm, feat_hbm, sup_hbm, dem_hbm, out,
            v_all, r, feat, sup, dem, z, w, top, acc, d, gain, m, s, tm, ms,
-           col, xbuf, zbuf, rowbuf, massown, massbuf, sp, fgive, fkeep, fmate, fsend, frecv,
+           col, xbuf, zbuf, rowbuf, massown, massbuf, sp, packed, fgive, fkeep, fmate, fsend, frecv,
            load_sem, ag_send, ag_recv, relay, x_send, x_recv, z_send, z_recv, row_sem, mass_sem,
            mate_send, mate_recv, f_send, f_recv):
     me, b = lax.axis_index("veh"), lax.axis_index("req")
@@ -153,8 +158,11 @@
     def at(dy, dc):
         return lax.rem(y + dy, NY) * 2 + lax.rem(core + dc, 2)
 
+    def place(q):
+        return at(q // 2, q % 2)
+
     loads = [
-        pltpu.make_async_copy(v_hbm, v_all.at[b], load_sem.at[0]),
+        pltpu.make_async_copy(v_hbm, v_all.at[0], load_sem.at[0]),
         pltpu.make_async_copy(r_hbm, r, load_sem.at[1]),
         pltpu.make_async_copy(sup_hbm, sup, load_sem.at[2]),
         pltpu.make_async_copy(dem_hbm, dem, load_sem.at[3]),
@@ -178,28 +186,34 @@
     def told(i):
         pl.semaphore_wait(relay.at[i], 2)
 
-    for dy, dc in ((2, 0), (2, 1), (1, 0), (3, 0), (1, 1), (3, 1), (0, 1)):
+    for q in (4, 5, 2, 6, 3, 7, 1):
+        dy, dc = q // 2, q % 2
+        there = (NY - dy) % NY * 2 + dc
         copy = pltpu.make_async_remote_copy(
-            v_all.at[b], v_all.at[b], ag_send.at[dy, dc], ag_recv.at[(NY - dy) % NY, dc],
+            v_all.at[0], v_all.at[there], ag_send.at[q], ag_recv.at[there],
             device_id=(me, at(dy, dc)), device_id_type=MESH)
         copy.start()
         sent.append(copy.wait_send)
     tell(0)
 
-    def arrival(dy, dc):
-        slot = at(dy, dc)
-        pltpu.make_async_copy(v_all.at[slot], v_all.at[slot], ag_recv.at[dy, dc]).wait()
-        return slot
+    def arrived(*blocks):
+        for q in blocks:
+            pltpu.make_async_copy(v_all.at[q], v_all.at[q], ag_recv.at[q]).wait()
 
     loads[1].wait()
-    score_rows(v_all, r, z, top, acc, b, scale, first=True)
-    for i, (dy, dc) in enumerate(((0, 1), (1, 0), (3, 0), (1, 1), (3, 1))):
-        score_rows(v_all, r, z, top, acc, arrival(dy, dc), scale)
-        if i < 3:
-            told(i)
-        if i < 2:
-            tell(i + 1)
-    far = (arrival(2, 0), arrival(2, 1))
+    score_rows(v_all, r, z, top, acc, 0, 1, scale, first=True)
+    told(0)
+    tell(1)
+    arrived(1)
+    score_rows(v_all, r, z, top, acc, 1, 1, scale)
+    told(1)
+    tell(2)
+    arrived(2, 3)
+    score_rows(v_all, r, z, top, acc, 2, 2, scale)
+    told(2)
+    arrived(6, 7)
+    score_rows(v_all, r, z, top, acc, 6, 2, scale)
+    arrived(4, 5)
 
     def x_start(a, c):
         for k in range(1, NX):
@@ -221,8 +235,7 @@
     loads[2].wait()
     loads[3].wait()
     for c in range(NCHUNK):
-        for slot in far:
-            score_rows(v_all, r, z, top, acc, slot, scale, start=c * cw, stop=(c + 1) * cw)
+        score_rows(v_all, r, z, top, acc, 4, 2, scale, start=c * cw, stop=(c + 1) * cw)
         xbuf[0, c, NX - 1] = column_lse(top, acc, pl.ds(c * cw, cw))
         x_start(0, c)
     for c in range(NCHUNK):
@@ -235,7 +248,7 @@
         d[:, cols] = dem[:, cols] * LOG2E - lse_parts(zbuf[0, c])
         row_pass(z, d, w, m, s, c, cw)
 
-    row_totals(m, s, rowbuf.at[NB - 1])
+    row_totals(m, s, rowbuf.at[NB - 1], place)
     for k in range(1, NB):
         pltpu.make_async_remote_copy(
             rowbuf.at[NB - 1], rowbuf.at[NB - 1 - k], row_sem.at[0], row_sem.at[1],
@@ -243,7 +256,7 @@
     sent.append(lambda: all_of(rowbuf, NB - 1, row_sem.at[0]))
     all_of(rowbuf, NB - 1, row_sem.at[1])
     sp[...] = sup[...] * LOG2E - lse_parts(rowbuf[...])
-    spread(sp, col)
+    spread(sp, col, place)
 
     for c in range(NCHUNK):
         xbuf[1, c, NX - 1] = column_sum(w, m, col, c, cw)
@@ -256,70 +269,64 @@
         all_of(zbuf.at[1, c], NZ - 1, z_recv.at[1, c])
         cols = pl.ds(c * cw, cw)
         gain[:, cols] = jnp.exp2(dem[:, cols] * LOG2E) / jnp.sum(zbuf[1, c], axis=0)
-        weight_pass(w, m, gain, z, tm, ms, c, cw)
-
-    def masses():
-        for g in range(NB):
-            massown[g] = jnp.sum(ms[pl.ds(g * BLK, BLK), :].T, axis=0, keepdims=True)
-        for k in range(1, NB):
-            pltpu.make_async_remote_copy(
-                massown.at[lax.rem(b + k, NB)], massbuf.at[NB - 1 - k], mass_sem.at[0], mass_sem.at[1],
-                device_id=req_peer(k), device_id_type=MESH).start()
-        sent.append(lambda: all_of(massbuf, NB - 1, mass_sem.at[0]))
-        massbuf[NB - 1] = massown[b]
-
-    def mate_copy(i):
+        weight_pass(w, m, gain, tm, ms, c, cw)
+
+    for q in range(NB):
+        massown[q] = jnp.sum(ms[pl.ds(q * BLK, BLK), :].T, axis=0, keepdims=True)
+    for q in range(1, NB):
+        there = (NY - q // 2) % NY * 2 + q % 2
+        pltpu.make_async_remote_copy(
+            massown.at[q], massbuf.at[there], mass_sem.at[0], mass_sem.at[1],
+            device_id=(me, place(q)), device_id_type=MESH).start()
+    others = massbuf.at[pl.ds(1, NB - 1)]
+    sent.append(lambda: pltpu.make_async_copy(others, others, mass_sem.at[0]).wait())
+    massbuf[0] = massown[0]
+
+    def mate_copy(dy):
         return pltpu.make_async_remote_copy(
-            fgive.at[i], fmate.at[i], mate_send.at[i], mate_recv.at[i],
+            fgive.at[dy], fmate.at[dy], mate_send.at[dy], mate_recv.at[dy],
             device_id=(me, at(0, 1)), device_id_type=MESH)
 
-    def out_copy(i):
+    def out_copy(dy):
         return pltpu.make_async_remote_copy(
-            fsend.at[i], frecv.at[i], f_send.at[i], f_recv.at[i],
-            device_id=(me, at(steps[i], 0)), device_id_type=MESH)
-
-    def give(i):
-        fgive[i] = block_features(z, tm, feat, at(steps[i], 1) * BLK, BLK)
-        mate_copy(i).start()
-        sent.append(mate_copy(i).wait_send)
-
-    def keep(i):
-        fkeep[i] = block_features(z, tm, feat, at(steps[i], 0) * BLK, BLK)
-
-    def pass_on(i):
-        mate_copy(i).wait_recv()
-        fsend[i] = (fkeep[i] + fmate[i]).astype(jnp.bfloat16)
-        out_copy(i).start()
-        sent.append(out_copy(i).wait_send)
-
-    steps = (2, 1, 3, 0)
-    last = len(steps) - 1
+            fsend.at[dy - 1], frecv.at[dy - 1], f_send.at[dy - 1], f_recv.at[dy - 1],
+            device_id=(me, at(dy, 0)), device_id_type=MESH)
+
+    def unit(dy, i):
+        f = block_features(w, m, gain, tm, feat, packed.at[i % 2], dy * 2 * BLK, 2 * BLK, cw)
+        fgive[dy] = f[BLK:]
+        mate_copy(dy).start()
+        fkeep[dy] = f[:BLK]
+
+    def pass_on(dy):
+        mate_copy(dy).wait_recv()
+        fsend[dy - 1] = (fkeep[dy] + fmate[dy]).astype(jnp.bfloat16)
+        out_copy(dy).start()
+
     loads[4].wait()
-    give(0)
-    give(1)
-    give(2)
-    keep(0)
-    masses()
-    keep(1)
-    pass_on(0)
-    keep(2)
+    unit(2, 0)
+    unit(1, 1)
+    pass_on(2)
+    unit(3, 2)
     pass_on(1)
-    give(3)
-    pass_on(2)
-    keep(3)
-    all_of(massbuf, NB - 1, mass_sem.at[1])
+    unit(0, 3)
+    pass_on(3)
+    for wait in sent:
+        wait()
+    pltpu.make_async_copy(others, others, mass_sem.at[1]).wait()
     mass = jnp.sum(massbuf[...], axis=0)
     inv = 1.0 / jnp.broadcast_to(mass, (BLK, LANES)).T
-    mate_copy(last).wait_recv()
-    total = fkeep[last] + fmate[last]
-    for i in (1, 2, 0):
-        out_copy(i).wait_recv()
-        total = total + frecv[i].astype(jnp.float32)
+    mate_copy(0).wait_recv()
+    total = fkeep[0] + fmate[0]
+    for dy in (1, 2, 3):
+        out_copy(dy).wait_recv()
+        total = total + frecv[dy - 1].astype(jnp.float32)
     for k in range(feat.shape[1] // LANES):
         out[:, k * LANES:(k + 1) * LANES] = total[:, k * LANES:(k + 1) * LANES] * inv
-
-    for wait in sent:
-        wait()
+    for dy in range(NY):
+        mate_copy(dy).wait_send()
+        if dy:
+            out_copy(dy).wait_send()
 
 
 def local(vehicle_emb, request_emb, request_feat, log_supply, log_demand):
@@ -350,12 +357,13 @@
         pltpu.VMEM((NB, 1, LANES), f32),
         pltpu.VMEM((NB, 1, LANES), f32),
         pltpu.VMEM((NB, 1, LANES), f32),
+        pltpu.VMEM((2, 2 * BLK, cols), bf16),
         pltpu.VMEM((NY, BLK, width), f32),
         pltpu.VMEM((NY, BLK, width), f32),
         pltpu.VMEM((NY, BLK, width), f32),
         pltpu.VMEM((NY - 1, BLK, width), bf16),
         pltpu.VMEM((NY - 1, BLK, width), bf16),
-        dma((5,)), dma((NY, 2)), dma((NY, 2)), pltpu.SemaphoreType.REGULAR((3,)),
+        dma((5,)), dma((NB,)), dma((NB,)), pltpu.SemaphoreType.REGULAR((3,)),
         dma((2, NCHUNK)), dma((2, NCHUNK)), dma((2, NCHUNK)), dma((2, NCHUNK)),
         dma((2,)), dma((2,)),
         dma((NY,)), dma((NY,)), dma((NY - 1,)), dma((NY - 1,)),

time: 55.8 us -> 55.1 us (0.987)
  Pallas kernels: 54 us -> 53.4 us
    pallas_call x1, Pallas kernels: 54 us -> 53.4 us  [local(): pl.pallas_call(kernel, out_shape=jax.ShapeDtypeStruct((BLK, width), f32),...]
where the time goes in v4:
time: 55.1 us; the launch traced here: 55 us
  Pallas kernels  53.4 us (97%)
  local copies, waits for them, and re-layouts  1.57 us (3%)
    pallas_call x1, Pallas kernels, local(): pl.pallas_call(kernel, out_shape=jax.ShapeDtypeStruct((BLK, width), f32),...  53.4 us
    unnamed x1, local copies, waits for them, and re-layouts  1.57 us

profile of v4, /device:TPU:1, one launch (start us, length us, event | category | flops | bytes accessed | tf_op | source)
XLA Modules:
  0.0 55.0 jit_solution(72341644271291594)
XLA Ops:
  0.0 53.4 %sinkhorn_assign.1 = f32[128,256]{1,0:T(8,128)} custom-call(bf16[128,128]{1,0:T(8,128)(2,1)} %v_hbm.1, bf16[4096,128]{1,0:T(8,128)(2,1)} %r_hbm.1, bf16[4096,256]{1,0:T(8,128)(2,1)} %feat_hbm.1, f32[8,1,128]{2,1,0:T(1,128)} %bitcast.3, f32[1,4096]{1,0:T(1,128)} %bitcast.2), custom_call_target="tpu_custom_call" | custom-call | flops 3221225472 | bytes 4194304 | tf_op jit(solution)/shard_map/sinkhorn_assign/pallas_call | solution.py:371
  53.5 1.6 %copy.7 = f32[128,256]{1,0:T(8,128)} copy(f32[128,256]{1,0:T(8,128)} %sinkhorn_assign.1) | data formatting | bytes 262144

commit v5 on v4

--- a/solution.py
+++ b/solution.py
@@ -95,8 +95,8 @@
     return jnp.concatenate([jnp.sum(a, axis=0, keepdims=True) for a in accs], axis=1)
 
 
-def weight_pass(w, u, gain, tm, ms, c, cw):
-    rows = 64
+def weight_pass(w, gain, tm, ms, c, cw):
+    rows = 32
     kk = cw // LANES
 
     def step(i, _):
@@ -107,27 +107,30 @@
             e = w[rr, cols] * gain[:, cols]
             peak = e if peak is None else jnp.maximum(peak, e)
             total = e if total is None else total + e
-        ut = u[c, rr, :]
-        peak, total = peak * ut, total * ut
-        if c > 0:
-            peak, total = jnp.maximum(peak, tm[rr, :]), total + ms[rr, :]
-        tm[rr, :] = peak
-        ms[rr, :] = total
+        tm[c, rr, :] = peak
+        ms[c, rr, :] = total
         return 0
 
-    lax.fori_loop(0, w.shape[0] // rows, step, 0)
-
-
-def block_features(w, u, gain, tm, feat, packed, row0, rows, cw):
+    lax.fori_loop(0, w.shape[0] // rows, step, 0, unroll=4)
+
+
+def block_mass(u, ms, row0):
+    rr = pl.ds(row0, BLK)
+    return jnp.sum(sum(ms[c, rr, :] * u[c, rr, :] for c in range(NCHUNK)).T, axis=0, keepdims=True)
+
+
+def block_features(w, u, gain, tm, feat, row0, rows, cw):
     rr = pl.ds(row0, rows)
-    peak = jnp.maximum(jnp.max(tm[rr, :], axis=1, keepdims=True), TINY)
+    peak = functools.reduce(jnp.maximum, [tm[c, rr, :] * u[c, rr, :] for c in range(NCHUNK)])
+    peak = jnp.maximum(jnp.max(peak, axis=1, keepdims=True), TINY)
     inv = 1.0 / peak
+    weights = []
     for c in range(NCHUNK):
         a = u[c, rr, :] * inv
         for k in range(cw // LANES):
             cols = pl.ds(c * cw + k * LANES, LANES)
-            packed[:, cols] = (w[rr, cols] * a * gain[:, cols]).astype(jnp.bfloat16)
-    return jnp.dot(packed[...], feat[...], preferred_element_type=jnp.float32) * peak
+            weights.append((w[rr, cols] * a * gain[:, cols]).astype(jnp.bfloat16))
+    return jnp.dot(jnp.concatenate(weights, axis=1), feat[...], preferred_element_type=jnp.float32) * peak
 
 
 def lse_parts(parts):
@@ -136,8 +139,8 @@
 
 
 def kernel(v_hbm, r_hbm, feat_hbm, sup_hbm, dem_hbm, out,
-           v_all, r, feat, sup, dem, z, w, top, acc, d, gain, m, s, tm, ms,
-           col, xbuf, zbuf, rowbuf, massown, massbuf, sp, packed, fgive, fkeep, fmate, fsend, frecv,
+           v_all, r, feat, sup, dem, z, w, top, acc, d, gain, m, s, tm,
+           col, xbuf, zbuf, rowbuf, massown, massbuf, sp, fgive, fkeep, fmate, fsend, frecv,
            load_sem, ag_send, ag_recv, relay, x_send, x_recv, z_send, z_recv, row_sem, mass_sem,
            mate_send, mate_recv, f_send, f_recv):
     me, b = lax.axis_index("veh"), lax.axis_index("req")
@@ -269,10 +272,10 @@
         all_of(zbuf.at[1, c], NZ - 1, z_recv.at[1, c])
         cols = pl.ds(c * cw, cw)
         gain[:, cols] = jnp.exp2(dem[:, cols] * LOG2E) / jnp.sum(zbuf[1, c], axis=0)
-        weight_pass(w, m, gain, tm, ms, c, cw)
+        weight_pass(w, gain, tm, s, c, cw)
 
     for q in range(NB):
-        massown[q] = jnp.sum(ms[pl.ds(q * BLK, BLK), :].T, axis=0, keepdims=True)
+        massown[q] = block_mass(m, s, q * BLK)
     for q in range(1, NB):
         there = (NY - q // 2) % NY * 2 + q % 2
         pltpu.make_async_remote_copy(
@@ -292,8 +295,8 @@
             fsend.at[dy - 1], frecv.at[dy - 1], f_send.at[dy - 1], f_recv.at[dy - 1],
             device_id=(me, at(dy, 0)), device_id_type=MESH)
 
-    def unit(dy, i):
-        f = block_features(w, m, gain, tm, feat, packed.at[i % 2], dy * 2 * BLK, 2 * BLK, cw)
+    def unit(dy):
+        f = block_features(w, m, gain, tm, feat, dy * 2 * BLK, 2 * BLK, cw)
         fgive[dy] = f[BLK:]
         mate_copy(dy).start()
         fkeep[dy] = f[:BLK]
@@ -304,12 +307,12 @@
         out_copy(dy).start()
 
     loads[4].wait()
-    unit(2, 0)
-    unit(1, 1)
+    unit(2)
+    unit(1)
     pass_on(2)
-    unit(3, 2)
+    unit(3)
     pass_on(1)
-    unit(0, 3)
+    unit(0)
     pass_on(3)
     for wait in sent:
         wait()
@@ -348,8 +351,7 @@
         pltpu.VMEM((1, cols), f32),
         pltpu.VMEM((NCHUNK, rows, LANES), f32),
         pltpu.VMEM((NCHUNK, rows, LANES), f32),
-        pltpu.VMEM((rows, LANES), f32),
-        pltpu.VMEM((rows, LANES), f32),
+        pltpu.VMEM((NCHUNK, rows, LANES), f32),
         pltpu.VMEM((rows, LANES), f32),
         pltpu.VMEM((2, NCHUNK, NX, 1, cw), f32),
         pltpu.VMEM((2, NCHUNK, NZ, 1, cw), f32),
@@ -357,7 +359,6 @@
         pltpu.VMEM((NB, 1, LANES), f32),
         pltpu.VMEM((NB, 1, LANES), f32),
         pltpu.VMEM((NB, 1, LANES), f32),
-        pltpu.VMEM((2, 2 * BLK, cols), bf16),
         pltpu.VMEM((NY, BLK, width), f32),
         pltpu.VMEM((NY, BLK, width), f32),
         pltpu.VMEM((NY, BLK, width), f32),

time: 55.1 us -> 54.2 us (0.984)
  Pallas kernels: 53.4 us -> 52.6 us
    pallas_call x1, Pallas kernels: 53.4 us -> 52.6 us  [local(): pl.pallas_call(kernel, out_shape=jax.ShapeDtypeStruct((BLK, width), f32),...]
where the time goes in v5:
time: 54.2 us
  Pallas kernels  52.6 us (97%)
  local copies, waits for them, and re-layouts  1.57 us (3%)
    pallas_call x1, Pallas kernels, local(): pl.pallas_call(kernel, out_shape=jax.ShapeDtypeStruct((BLK, width), f32),...  52.6 us
    unnamed x1, local copies, waits for them, and re-layouts  1.57 us

profile of v5, /device:TPU:1, one launch (start us, length us, event | category | flops | bytes accessed | tf_op | source)
XLA Modules:
  0.0 54.2 jit_solution(5906258910805389596)
XLA Ops:
  0.0 52.6 %sinkhorn_assign.1 = f32[128,256]{1,0:T(8,128)} custom-call(bf16[128,128]{1,0:T(8,128)(2,1)} %v_hbm.1, bf16[4096,128]{1,0:T(8,128)(2,1)} %r_hbm.1, bf16[4096,256]{1,0:T(8,128)(2,1)} %feat_hbm.1, f32[8,1,128]{2,1,0:T(1,128)} %bitcast.3, f32[1,4096]{1,0:T(1,128)} %bitcast.2), custom_call_target="tpu_custom_call" | custom-call | flops 3221225472 | bytes 4194304 | tf_op jit(solution)/shard_map/sinkhorn_assign/pallas_call | solution.py:372
  52.6 1.6 %copy.7 = f32[128,256]{1,0:T(8,128)} copy(f32[128,256]{1,0:T(8,128)} %sinkhorn_assign.1) | data formatting | bytes 262144

commit v6 on v5

--- a/solution.py
+++ b/solution.py
@@ -177,7 +177,7 @@
     near_z = (z_peer(1), z_peer(NZ - 1))
     for peer in [req_peer(k) for k in range(1, NB)] + [x_peer(k) for k in range(1, NX)] + list(near_z):
         pl.semaphore_signal(barrier, inc=1, device_id=peer, device_id_type=MESH)
-    for load in loads[1:]:
+    for load in loads[1:4]:
         load.start()
     loads[0].wait()
     pl.semaphore_wait(barrier, NB - 1 + NX - 1 + 2)
@@ -204,6 +204,7 @@
             pltpu.make_async_copy(v_all.at[q], v_all.at[q], ag_recv.at[q]).wait()
 
     loads[1].wait()
+    loads[4].start()
     score_rows(v_all, r, z, top, acc, 0, 1, scale, first=True)
     told(0)
     tell(1)
@@ -274,6 +275,33 @@
         gain[:, cols] = jnp.exp2(dem[:, cols] * LOG2E) / jnp.sum(zbuf[1, c], axis=0)
         weight_pass(w, gain, tm, s, c, cw)
 
+    def mate_copy(dy):
+        return pltpu.make_async_remote_copy(
+            fgive.at[dy], fmate.at[dy], mate_send.at[dy], mate_recv.at[dy],
+            device_id=(me, at(0, 1)), device_id_type=MESH)
+
+    def out_copy(dy):
+        return pltpu.make_async_remote_copy(
+            fsend.at[dy - 1], frecv.at[dy - 1], f_send.at[dy - 1], f_recv.at[dy - 1],
+            device_id=(me, at(dy, 0)), device_id_type=MESH)
+
+    def unit(dy):
+        f = block_features(w, m, gain, tm, feat, dy * 2 * BLK, 2 * BLK, cw)
+        fgive[dy] = f[BLK:]
+        mate_copy(dy).start()
+        fkeep[dy] = f[:BLK]
+
+    def pass_on(dy):
+        mate_copy(dy).wait_recv()
+        fsend[dy - 1] = (fkeep[dy] + fmate[dy]).astype(jnp.bfloat16)
+        out_copy(dy).start()
+
+    loads[4].wait()
+    unit(2)
+    unit(1)
+    pass_on(2)
+    unit(3)
+    pass_on(1)
     for q in range(NB):
         massown[q] = block_mass(m, s, q * BLK)
     for q in range(1, NB):
@@ -285,35 +313,8 @@
     sent.append(lambda: pltpu.make_async_copy(others, others, mass_sem.at[0]).wait())
     massbuf[0] = massown[0]
 
-    def mate_copy(dy):
-        return pltpu.make_async_remote_copy(
-            fgive.at[dy], fmate.at[dy], mate_send.at[dy], mate_recv.at[dy],
-            device_id=(me, at(0, 1)), device_id_type=MESH)
-
-    def out_copy(dy):
-        return pltpu.make_async_remote_copy(
-            fsend.at[dy - 1], frecv.at[dy - 1], f_send.at[dy - 1], f_recv.at[dy - 1],
-            device_id=(me, at(dy, 0)), device_id_type=MESH)
-
-    def unit(dy):
-        f = block_features(w, m, gain, tm, feat, dy * 2 * BLK, 2 * BLK, cw)
-        fgive[dy] = f[BLK:]
-        mate_copy(dy).start()
-        fkeep[dy] = f[:BLK]
-
-    def pass_on(dy):
-        mate_copy(dy).wait_recv()
-        fsend[dy - 1] = (fkeep[dy] + fmate[dy]).astype(jnp.bfloat16)
-        out_copy(dy).start()
-
-    loads[4].wait()
-    unit(2)
-    unit(1)
-    pass_on(2)
-    unit(3)
-    pass_on(1)
+    pass_on(3)
     unit(0)
-    pass_on(3)
     for wait in sent:
         wait()
     pltpu.make_async_copy(others, others, mass_sem.at[1]).wait()
@@ -371,8 +372,8 @@
     ]
     return pl.pallas_call(
         kernel,
-        out_shape=jax.ShapeDtypeStruct((BLK, width), f32),
-        in_specs=[pl.BlockSpec(memory_space=pl.ANY)] * 5,
+        out_shape=pltpu.VMEM((BLK, width), f32),
+        in_specs=[pl.BlockSpec(memory_space=pltpu.HBM)] * 5,
         out_specs=pl.BlockSpec(memory_space=pltpu.VMEM),
         scratch_shapes=scratch,
         compiler_params=pltpu.CompilerParams(

time: 54.2 us -> 52.7 us (0.972)
  local copies, waits for them, and re-layouts: 1.57 us -> 0.66 us
  Pallas kernels: 52.6 us -> 51.9 us
    unnamed x1, local copies, waits for them, and re-layouts: 1.57 us -> 0.66 us
    pallas_call x1, Pallas kernels: 52.6 us -> 51.9 us  [local(): pl.pallas_call(kernel, out_shape=pltpu.VMEM((BLK, width), f32), in_specs=...]
where the time goes in v6:
time: 52.7 us; the launch traced here: 52.6 us
  Pallas kernels  51.9 us (98%)
  local copies, waits for them, and re-layouts  0.66 us (1%)
    pallas_call x1, Pallas kernels, local(): pl.pallas_call(kernel, out_shape=pltpu.VMEM((BLK, width), f32), in_specs=...  51.9 us

profile of v6, /device:TPU:1, one launch (start us, length us, event | category | flops | bytes accessed | tf_op | source)
XLA Modules:
  0.0 52.6 jit_solution(13372095776553950)
XLA Ops:
  0.0 51.9 %sinkhorn_assign.1 = f32[128,256]{1,0:T(8,128)S(1)} custom-call(bf16[128,128]{1,0:T(8,128)(2,1)} %v_hbm.1, bf16[4096,128]{1,0:T(8,128)(2,1)} %r_hbm.1, bf16[4096,256]{1,0:T(8,128)(2,1)} %feat_hbm.1, f32[8,1,128]{2,1,0:T(1,128)} %bitcast.3, f32[1,4096]{1,0:T(1,128)} %bitcast.2), custom_call_target="tpu_custom_call" | custom-call | flops 3221225472 | bytes 4194304 | tf_op jit(solution)/shard_map/sinkhorn_assign/pallas_call | solution.py:373
  52.0 0.7 %copy.7 = f32[128,256]{1,0:T(8,128)} copy(f32[128,256]{1,0:T(8,128)S(1)} %sinkhorn_assign.1) | data formatting | bytes 262144

commit v7 on v6

--- a/solution.py
+++ b/solution.py
@@ -172,14 +172,12 @@
         pltpu.make_async_copy(feat_hbm, feat, load_sem.at[4]),
     ]
     sent = []
-    loads[0].start()
     barrier = pltpu.get_barrier_semaphore()
     near_z = (z_peer(1), z_peer(NZ - 1))
     for peer in [req_peer(k) for k in range(1, NB)] + [x_peer(k) for k in range(1, NX)] + list(near_z):
         pl.semaphore_signal(barrier, inc=1, device_id=peer, device_id_type=MESH)
-    for load in loads[1:4]:
+    for load in loads[:4]:
         load.start()
-    loads[0].wait()
     pl.semaphore_wait(barrier, NB - 1 + NX - 1 + 2)
 
     def tell(i):
@@ -193,7 +191,7 @@
         dy, dc = q // 2, q % 2
         there = (NY - dy) % NY * 2 + dc
         copy = pltpu.make_async_remote_copy(
-            v_all.at[0], v_all.at[there], ag_send.at[q], ag_recv.at[there],
+            v_hbm, v_all.at[there], ag_send.at[q], ag_recv.at[there],
             device_id=(me, at(dy, dc)), device_id_type=MESH)
         copy.start()
         sent.append(copy.wait_send)
@@ -203,6 +201,7 @@
         for q in blocks:
             pltpu.make_async_copy(v_all.at[q], v_all.at[q], ag_recv.at[q]).wait()
 
+    loads[0].wait()
     loads[1].wait()
     loads[4].start()
     score_rows(v_all, r, z, top, acc, 0, 1, scale, first=True)
@@ -220,14 +219,14 @@
     arrived(4, 5)
 
     def x_start(a, c):
-        for k in range(1, NX):
+        for k in (2, 1, 3):
             pltpu.make_async_remote_copy(
                 xbuf.at[a, c, NX - 1], xbuf.at[a, c, NX - 1 - k], x_send.at[a, c], x_recv.at[a, c],
                 device_id=x_peer(k), device_id_type=MESH).start()
         sent.append(lambda: all_of(xbuf.at[a, c], NX - 1, x_send.at[a, c]))
 
     def z_start(a, c):
-        for k in range(1, NZ):
+        for k in (4, 3, 5, 2, 6, 1, 7):
             pltpu.make_async_remote_copy(
                 zbuf.at[a, c, NZ - 1], zbuf.at[a, c, NZ - 1 - k], z_send.at[a, c], z_recv.at[a, c],
                 device_id=z_peer(k), device_id_type=MESH).start()
@@ -253,7 +252,7 @@
         row_pass(z, d, w, m, s, c, cw)
 
     row_totals(m, s, rowbuf.at[NB - 1], place)
-    for k in range(1, NB):
+    for k in (4, 3, 5, 2, 6, 1, 7):
         pltpu.make_async_remote_copy(
             rowbuf.at[NB - 1], rowbuf.at[NB - 1 - k], row_sem.at[0], row_sem.at[1],
             device_id=req_peer(k), device_id_type=MESH).start()

time: 52.7 us -> 53 us (level)
  no operation moved by 1% of the time
where the time goes in v7:
time: 53 us; the launch traced here: 52.9 us
  Pallas kernels  52.3 us (99%)
  local copies, waits for them, and re-layouts  0.66 us (1%)
    pallas_call x1, Pallas kernels, local(): pl.pallas_call(kernel, out_shape=pltpu.VMEM((BLK, width), f32), in_specs=...  52.3 us

profile of v7, /device:TPU:1, one launch (start us, length us, event | category | flops | bytes accessed | tf_op | source)
XLA Modules:
  0.0 52.9 jit_solution(2088139992146372359)
XLA Ops:
  0.0 52.3 %sinkhorn_assign.1 = f32[128,256]{1,0:T(8,128)S(1)} custom-call(bf16[128,128]{1,0:T(8,128)(2,1)} %v_hbm.1, bf16[4096,128]{1,0:T(8,128)(2,1)} %r_hbm.1, bf16[4096,256]{1,0:T(8,128)(2,1)} %feat_hbm.1, f32[8,1,128]{2,1,0:T(1,128)} %bitcast.3, f32[1,4096]{1,0:T(1,128)} %bitcast.2), custom_call_target="tpu_custom_call" | custom-call | flops 3221225472 | bytes 4194304 | tf_op jit(solution)/shard_map/sinkhorn_assign/pallas_call | solution.py:372
  52.3 0.7 %copy.7 = f32[128,256]{1,0:T(8,128)} copy(f32[128,256]{1,0:T(8,128)S(1)} %sinkhorn_assign.1) | data formatting | bytes 262144

commit v8 on v7

--- a/solution.py
+++ b/solution.py
@@ -187,7 +187,7 @@
     def told(i):
         pl.semaphore_wait(relay.at[i], 2)
 
-    for q in (4, 5, 2, 6, 3, 7, 1):
+    for q in (1, 2, 3, 4, 5, 6, 7):
         dy, dc = q // 2, q % 2
         there = (NY - dy) % NY * 2 + dc
         copy = pltpu.make_async_remote_copy(
@@ -214,9 +214,7 @@
     arrived(2, 3)
     score_rows(v_all, r, z, top, acc, 2, 2, scale)
     told(2)
-    arrived(6, 7)
-    score_rows(v_all, r, z, top, acc, 6, 2, scale)
-    arrived(4, 5)
+    arrived(4, 5, 6, 7)
 
     def x_start(a, c):
         for k in (2, 1, 3):
@@ -238,7 +236,7 @@
     loads[2].wait()
     loads[3].wait()
     for c in range(NCHUNK):
-        score_rows(v_all, r, z, top, acc, 4, 2, scale, start=c * cw, stop=(c + 1) * cw)
+        score_rows(v_all, r, z, top, acc, 4, 4, scale, start=c * cw, stop=(c + 1) * cw)
         xbuf[0, c, NX - 1] = column_lse(top, acc, pl.ds(c * cw, cw))
         x_start(0, c)
     for c in range(NCHUNK):

time: 53 us -> 51.9 us (0.979)
  Pallas kernels: 52.3 us -> 51.1 us
    pallas_call x1, Pallas kernels: 52.3 us -> 51.1 us  [local(): pl.pallas_call(kernel, out_shape=pltpu.VMEM((BLK, width), f32), in_specs=...]
where the time goes in v8:
time: 51.9 us; the launch traced here: 51.8 us
  Pallas kernels  51.1 us (98%)
  local copies, waits for them, and re-layouts  0.66 us (1%)
    pallas_call x1, Pallas kernels, local(): pl.pallas_call(kernel, out_shape=pltpu.VMEM((BLK, width), f32), in_specs=...  51.1 us

profile of v8, /device:TPU:1, one launch (start us, length us, event | category | flops | bytes accessed | tf_op | source)
XLA Modules:
  0.0 51.8 jit_solution(2009158563324686681)
XLA Ops:
  0.0 51.1 %sinkhorn_assign.1 = f32[128,256]{1,0:T(8,128)S(1)} custom-call(bf16[128,128]{1,0:T(8,128)(2,1)} %v_hbm.1, bf16[4096,128]{1,0:T(8,128)(2,1)} %r_hbm.1, bf16[4096,256]{1,0:T(8,128)(2,1)} %feat_hbm.1, f32[8,1,128]{2,1,0:T(1,128)} %bitcast.3, f32[1,4096]{1,0:T(1,128)} %bitcast.2), custom_call_target="tpu_custom_call" | custom-call | flops 3221225472 | bytes 4194304 | tf_op jit(solution)/shard_map/sinkhorn_assign/pallas_call | solution.py:370
  51.2 0.7 %copy.7 = f32[128,256]{1,0:T(8,128)} copy(f32[128,256]{1,0:T(8,128)S(1)} %sinkhorn_assign.1) | data formatting | bytes 262144

commit v9 on v8

--- a/solution.py
+++ b/solution.py
@@ -166,7 +166,7 @@
 
     loads = [
         pltpu.make_async_copy(v_hbm, v_all.at[0], load_sem.at[0]),
-        pltpu.make_async_copy(r_hbm, r, load_sem.at[1]),
+        pltpu.make_async_copy(r_hbm.at[pl.ds(0, cw)], r.at[pl.ds(0, cw)], load_sem.at[1]),
         pltpu.make_async_copy(sup_hbm, sup, load_sem.at[2]),
         pltpu.make_async_copy(dem_hbm, dem, load_sem.at[3]),
         pltpu.make_async_copy(feat_hbm, feat, load_sem.at[4]),
@@ -176,7 +176,11 @@
     near_z = (z_peer(1), z_peer(NZ - 1))
     for peer in [req_peer(k) for k in range(1, NB)] + [x_peer(k) for k in range(1, NX)] + list(near_z):
         pl.semaphore_signal(barrier, inc=1, device_id=peer, device_id_type=MESH)
-    for load in loads[:4]:
+    more = [
+        pltpu.make_async_copy(r_hbm.at[pl.ds(c * cw, cw)], r.at[pl.ds(c * cw, cw)], load_sem.at[4 + c])
+        for c in range(1, NCHUNK)
+    ]
+    for load in loads[:2] + more + loads[2:4]:
         load.start()
     pl.semaphore_wait(barrier, NB - 1 + NX - 1 + 2)
 
@@ -202,9 +206,10 @@
             pltpu.make_async_copy(v_all.at[q], v_all.at[q], ag_recv.at[q]).wait()
 
     loads[0].wait()
-    loads[1].wait()
+    for c, load in enumerate([loads[1]] + more):
+        load.wait()
+        score_rows(v_all, r, z, top, acc, 0, 1, scale, first=True, start=c * cw, stop=(c + 1) * cw)
     loads[4].start()
-    score_rows(v_all, r, z, top, acc, 0, 1, scale, first=True)
     told(0)
     tell(1)
     arrived(1)
@@ -362,7 +367,7 @@
         pltpu.VMEM((NY, BLK, width), f32),
         pltpu.VMEM((NY - 1, BLK, width), bf16),
         pltpu.VMEM((NY - 1, BLK, width), bf16),
-        dma((5,)), dma((NB,)), dma((NB,)), pltpu.SemaphoreType.REGULAR((3,)),
+        dma((4 + NCHUNK,)), dma((NB,)), dma((NB,)), pltpu.SemaphoreType.REGULAR((3,)),
         dma((2, NCHUNK)), dma((2, NCHUNK)), dma((2, NCHUNK)), dma((2, NCHUNK)),
         dma((2,)), dma((2,)),
         dma((NY,)), dma((NY,)), dma((NY - 1,)), dma((NY - 1,)),

time: 51.9 us -> 52 us (level)
  no operation moved by 1% of the time
where the time goes in v9:
time: 52 us; the launch traced here: 51.9 us
  Pallas kernels  51.3 us (99%)
  local copies, waits for them, and re-layouts  0.66 us (1%)
    pallas_call x1, Pallas kernels, local(): pl.pallas_call(kernel, out_shape=pltpu.VMEM((BLK, width), f32), in_specs=...  51.3 us

profile of v9, /device:TPU:1, one launch (start us, length us, event | category | flops | bytes accessed | tf_op | source)
XLA Modules:
  0.0 51.9 jit_solution(9763272514024512625)
XLA Ops:
  0.0 51.3 %sinkhorn_assign.1 = f32[128,256]{1,0:T(8,128)S(1)} custom-call(bf16[128,128]{1,0:T(8,128)(2,1)} %v_hbm.1, bf16[4096,128]{1,0:T(8,128)(2,1)} %r_hbm.1, bf16[4096,256]{1,0:T(8,128)(2,1)} %feat_hbm.1, f32[8,1,128]{2,1,0:T(1,128)} %bitcast.3, f32[1,4096]{1,0:T(1,128)} %bitcast.2), custom_call_target="tpu_custom_call" | custom-call | flops 3221225472 | bytes 4194304 | tf_op jit(solution)/shard_map/sinkhorn_assign/pallas_call | solution.py:375
  51.3 0.7 %copy.7 = f32[128,256]{1,0:T(8,128)} copy(f32[128,256]{1,0:T(8,128)S(1)} %sinkhorn_assign.1) | data formatting | bytes 262144
